TPU v7x, 128 devices: a whole 4x4x4 slice. The times are simulated.
128 devices in a mesh: cuts: 4 (over z), dp: 32 (over x, y, core).
Axes of the slice: x: 4, y: 4, z: 4, core: 2. Of those that a mesh axis runs over, the one named last changes fastest.
Arguments:
- hidden: bfloat16 [49152, 8192], P(('cuts', 'dp')), may hold values from -24 to 24
- kv_weight: bfloat16 [8192, 256], P(('cuts', 'dp')), may hold values from -0.0625 to 0.0625
- queries: bfloat16 [49152, 1024], P(('cuts', 'dp')), may hold values from -102 to 102
- out_grad: bfloat16 [49152, 1024], P(('cuts', 'dp')), may hold values from -6 to 6
- lengths: int32 [264], replicated, may hold values from 0 to 1536, as said below
Outputs:
- attended: bfloat16 [49152, 1024], P(('cuts', 'dp'))
- query_grad: bfloat16 [49152, 1024], P(('cuts', 'dp'))
- weight_grad: float32 [8192, 256], P(('cuts', 'dp'))
Inputs may be any that keep to these rules, and one draw needn't show every extreme that they name: Taken in order, the entries are the lengths of consecutive documents of the whole stream and sum to 49152; a zero entry is an empty document; the longest document has exactly 1536 tokens.
All inputs are finite; a program needn't handle non-finite values.
Results may differ from a plain program's by a relative error of at most 0.04.
The roundings to bfloat16 on the way count: a program that leaves them out, or rounds other values in their place, can miss the bound.
Values may be sent and summed in bfloat16 or wider, within the bound.
No kernel may reach another device: no remote copies, remote signals or barrier semaphores. Data moves between devices by JAX's collectives and lax.ppermute only.
A program may use at most 128 MiB of HBM per device.

v0:
```python
import functools
import math

import jax
import jax.numpy as jnp
from jax import lax
from jax.experimental import pallas as pl
from jax.experimental.pallas import tpu as pltpu
from jax.sharding import Mesh, PartitionSpec as P

SPAN = 4
NEG = -1e30
CHIPS = ("z", "x", "y")
ALL = ("z", "x", "y", "core")
SWAP = [(0, 1), (1, 0)]
CHUNKS = 4
VMEM = 56 * 1024 * 1024
BF = jnp.bfloat16
F32 = jnp.float32


def mm(a, b):
    return jnp.dot(a, b, preferred_element_type=F32)


def away_kernel(pick_ref, x_ref, away_ref):
    for n in range(x_ref.shape[1] // 256):
        y = mm(x_ref[:, n * 256 : (n + 1) * 256], pick_ref[...])
        away_ref[:, n * 128 : (n + 1) * 128] = y.astype(BF)


def keep_kernel(pick_ref, x_ref, keep_ref, turned_ref):
    for n in range(x_ref.shape[1] // 256):
        y = mm(x_ref[:, n * 256 : (n + 1) * 256], pick_ref[...]).astype(BF)
        keep_ref[:, n * 128 : (n + 1) * 128] = y
        turned_ref[n * 128 : (n + 1) * 128, :] = y.T


def join_kernel(*refs):
    parts, (whole_ref, turned_ref) = refs[:-2], refs[-2:]
    at = 0
    for part in parts:
        for n in range(0, part.shape[1], 128):
            y = part[:, n : n + 128]
            whole_ref[:, at : at + 128] = y
            turned_ref[at : at + 128, :] = y.T
            at += 128


def share_kernel(keep_ref, came_ref, mine_ref, other_ref, share_ref):
    share_ref[...] = (mm(keep_ref[...], mine_ref[...]) + mm(came_ref[...], other_ref[...])).astype(BF)


def params():
    return pltpu.CompilerParams(vmem_limit_bytes=VMEM)


def picker(side, part):
    out = jnp.arange(128, dtype=jnp.int32)
    source = (out // part) * 2 * part + side * part + out % part
    return (jnp.arange(256, dtype=jnp.int32)[:, None] == source[None, :]).astype(BF)


def away_columns(hidden, pick, chunk, chunks):
    rows, width = hidden.shape
    block = width // (2 * chunks)
    return pl.pallas_call(
        away_kernel,
        grid=(2,),
        in_specs=[
            pl.BlockSpec((256, 128), lambda i: (0, 0)),
            pl.BlockSpec((rows, block), lambda i: (0, 2 * chunk + i)),
        ],
        out_specs=pl.BlockSpec((rows, block // 2), lambda i: (0, i)),
        out_shape=jax.ShapeDtypeStruct((rows, block), BF),
        cost_estimate=pl.CostEstimate(flops=0, bytes_accessed=6 * rows * block, transcendentals=0),
        compiler_params=params(),
        name="away_columns",
    )(pick, hidden)


def kept_columns(hidden, pick):
    rows, width = hidden.shape
    block = 1024
    return pl.pallas_call(
        keep_kernel,
        grid=(width // block,),
        in_specs=[
            pl.BlockSpec((256, 128), lambda i: (0, 0)),
            pl.BlockSpec((rows, block), lambda i: (0, i)),
        ],
        out_specs=[
            pl.BlockSpec((rows, block // 2), lambda i: (0, i)),
            pl.BlockSpec((block // 2, rows), lambda i: (i, 0)),
        ],
        out_shape=[jax.ShapeDtypeStruct((rows, width // 2), BF), jax.ShapeDtypeStruct((width // 2, rows), BF)],
        cost_estimate=pl.CostEstimate(flops=0, bytes_accessed=6 * rows * width, transcendentals=0),
        compiler_params=params(),
        name="kept_columns",
    )(pick, hidden)


def joined(parts):
    rows, width = parts[0].shape[0], sum(part.shape[1] for part in parts)
    return pl.pallas_call(
        join_kernel,
        out_shape=[jax.ShapeDtypeStruct((rows, width), BF), jax.ShapeDtypeStruct((width, rows), BF)],
        cost_estimate=pl.CostEstimate(flops=0, bytes_accessed=8 * rows * width, transcendentals=0),
        compiler_params=params(),
        name="joined",
    )(*parts)


def chip_share(keep_t, came_t, mine, other):
    height, rows = keep_t.shape
    pair = mine.shape[1]
    block = 512
    return pl.pallas_call(
        share_kernel,
        grid=(height // block,),
        in_specs=[
            pl.BlockSpec((block, rows), lambda i: (i, 0)),
            pl.BlockSpec((block, rows), lambda i: (i, 0)),
            pl.BlockSpec((rows, pair), lambda i: (0, 0)),
            pl.BlockSpec((rows, pair), lambda i: (0, 0)),
        ],
        out_specs=pl.BlockSpec((block, pair), lambda i: (i, 0)),
        out_shape=jax.ShapeDtypeStruct((height, pair), BF),
        cost_estimate=pl.CostEstimate(flops=4 * height * rows * pair, bytes_accessed=6 * height * rows, transcendentals=0),
        compiler_params=params(),
        name="chip_share",
    )(keep_t, came_t, mine, other)


def key_chunks(rows):
    edge, span = 2 * rows // 3, (SPAN + 1) * rows
    chunks = [(0, edge, 0, edge)]
    at = edge
    while at < span - edge:
        end = min(at + 768, span - edge)
        chunks.append((at, end, 0, rows))
        at = end
    chunks.append((span - edge, span, rows - edge, rows))
    return chunks


def onto_rows(total, extra, first, end):
    parts = [total[:first], total[first:end] + extra, total[end:]]
    return jnp.concatenate([part for part in parts if part.shape[0]], axis=0)


def lane_groups(block, size):
    return [block[:, n : n + size] for n in range(0, block.shape[1], size)]


def attention_kernel(low_ref, q_ref, g_ref, *refs):
    pieces = refs[: SPAN + 1]
    out_ref, dq_ref, swap_ref, rest_ref, kv_ref, turned_ref, bias_ref, s_ref, p_ref, acc_ref = refs[SPAN + 1 :]
    step = pl.program_id(0)
    rows = q_ref.shape[0]
    size = kv_ref.shape[1] // 2
    span = kv_ref.shape[0]
    chunks = key_chunks(rows)
    scale = 1.0 / math.sqrt(size)
    scale2 = scale * math.log2(math.e)

    @pl.when(step == 0)
    def _():
        low = low_ref[:, :1]
        row = lax.broadcasted_iota(jnp.int32, (rows, rows), 0)
        for j, piece in enumerate(pieces):
            cols = slice(j * rows, (j + 1) * rows)
            kv_ref[cols, :] = piece[...]
            turned_ref[:size, cols] = piece[:, :size].T
            turned_ref[size:, cols] = piece[:, size:].T
            at = lax.broadcasted_iota(jnp.int32, (rows, rows), 1) + j * rows
            allowed = (at >= low) & (at <= row + SPAN * rows)
            bias_ref[:, cols] = jnp.where(allowed, 0.0, NEG)
        acc_ref[...] = jnp.zeros_like(acc_ref)

    heads = q_ref.shape[1] // size
    for h in range(heads):
        lanes = slice(h * size, (h + 1) * size)
        q = q_ref[:, lanes]
        top = jnp.full((rows, size), NEG, F32)
        for c0, c1, r0, r1 in chunks:
            s = mm(q[r0:r1], turned_ref[:size, c0:c1]) + bias_ref[r0:r1, c0:c1]
            s_ref[h, r0:r1, c0:c1] = s
            most = functools.reduce(jnp.maximum, lane_groups(s, size))
            parts = [top[:r0], jnp.maximum(top[r0:r1], most), top[r1:]]
            top = jnp.concatenate([part for part in parts if part.shape[0]], axis=0)
        peak = jnp.max(top, axis=1, keepdims=True) * scale2
        total = jnp.zeros((rows, size), F32)
        out = jnp.zeros((rows, size), F32)
        for c0, c1, r0, r1 in chunks:
            e = jnp.exp2(s_ref[h, r0:r1, c0:c1] * scale2 - peak[r0:r1])
            total = onto_rows(total, functools.reduce(jnp.add, lane_groups(e, size)), r0, r1)
            p = e.astype(BF)
            p_ref[h, r0:r1, c0:c1] = p
            out = onto_rows(out, mm(p, kv_ref[c0:c1, size:]), r0, r1)
        inverse = 1.0 / jnp.sum(total, axis=1, keepdims=True)
        out = out * inverse
        out_ref[:, lanes] = out.astype(BF)
        scaled = g_ref[:, lanes].astype(F32) * inverse
        g = scaled.astype(BF)
        delta = jnp.sum(g.astype(F32) * out, axis=1, keepdims=True)
        g_turned = scaled.T.astype(BF)
        q_turned = q.astype(F32).T.astype(BF)
        dq = jnp.zeros((rows, size), F32)
        for c0, c1, r0, r1 in chunks:
            p = p_ref[h, r0:r1, c0:c1]
            acc_ref[size:, c0:c1] += mm(g_turned[:, r0:r1], p)
            dp = mm(g[r0:r1], turned_ref[size:, c0:c1]) - delta[r0:r1]
            ds = dp.astype(BF) * p
            dq = onto_rows(dq, mm(ds, kv_ref[c0:c1, :size]), r0, r1)
            acc_ref[:size, c0:c1] += mm(q_turned[:, r0:r1], ds)
        dq_ref[:, lanes] = (dq * scale).astype(BF)

    @pl.when(step == pl.num_programs(0) - 1)
    def _():
        for j in range(SPAN + 1):
            cols = slice(j * rows, (j + 1) * rows)
            into = rest_ref.at[j // 2] if j % 2 == 0 else swap_ref.at[1 - j // 2]
            into[:, :size] = (acc_ref[:size, cols].T * scale).astype(BF)
            into[:, size:] = acc_ref[size:, cols].T.astype(BF)


HEADS_PER_STEP = 2


def attention(low, queries, out_grad, pieces):
    rows, width = queries.shape
    pair = pieces[0].shape[1]
    size = pair // 2
    heads = width // size
    span = (SPAN + 1) * rows
    several = pl.BlockSpec((rows, HEADS_PER_STEP * size), lambda h: (0, h))
    whole = pl.BlockSpec((rows, pair), lambda h: (0, 0))
    return pl.pallas_call(
        attention_kernel,
        grid=(heads // HEADS_PER_STEP,),
        in_specs=[pl.BlockSpec((rows, size), lambda h: (0, 0)), several, several] + [whole] * (SPAN + 1),
        out_specs=[
            several,
            several,
            pl.BlockSpec((SPAN // 2, rows, pair), lambda h: (0, 0, 0)),
            pl.BlockSpec((SPAN // 2 + 1, rows, pair), lambda h: (0, 0, 0)),
        ],
        out_shape=[
            jax.ShapeDtypeStruct((rows, width), BF),
            jax.ShapeDtypeStruct((rows, width), BF),
            jax.ShapeDtypeStruct((SPAN // 2, rows, pair), BF),
            jax.ShapeDtypeStruct((SPAN // 2 + 1, rows, pair), BF),
        ],
        scratch_shapes=[
            pltpu.VMEM((span, pair), BF),
            pltpu.VMEM((pair, span), BF),
            pltpu.VMEM((rows, span), F32),
            pltpu.VMEM((HEADS_PER_STEP, rows, span), F32),
            pltpu.VMEM((HEADS_PER_STEP, rows, span), BF),
            pltpu.VMEM((pair, span), F32),
        ],
        cost_estimate=pl.CostEstimate(
            flops=24 * heads * rows * span * size, bytes_accessed=10 * rows * width, transcendentals=heads * rows * span
        ),
        compiler_params=params(),
        name="attention",
    )(low, queries, out_grad, *pieces)


def between_cores(block):
    return lax.ppermute(block, "core", SWAP)


def between_chips(block, distance):
    devices = range(lax.axis_size(ALL))
    route = [(i, i + 2 * distance) for i in devices if i + 2 * distance in devices]
    return lax.ppermute(block, ALL, route)


def window_pieces(key_value, core):
    second = between_chips(key_value, 1)
    fourth = between_chips(key_value, 2)
    first = between_cores(jnp.where(core == 0, key_value, second))
    third = between_cores(jnp.where(core == 0, second, fourth))
    return [fourth, third, second, first, key_value]


def returned(swap, rest, core):
    came = between_cores(swap)
    first, third = came[0].astype(F32), came[1].astype(F32)
    near = (rest[1].astype(F32) + jnp.where(core == 0, third, first)).astype(BF)
    far = (rest[0].astype(F32) + jnp.where(core == 0, 0.0, third)).astype(BF)
    own = rest[2].astype(F32) + jnp.where(core == 0, first, 0.0)
    summed = own + between_chips(near, -1).astype(F32) + between_chips(far, -2).astype(F32)
    mine = summed.astype(BF)
    return mine, between_cores(mine)


def per_device(hidden, kv_weight, queries, out_grad, lengths):
    rows = hidden.shape[0]
    part, pair = kv_weight.shape
    core = lax.axis_index("core")
    chips = lax.axis_size(CHIPS)

    copies = jnp.broadcast_to(kv_weight[None], (chips, part, pair))
    weight = lax.all_to_all(copies, CHIPS, 0, 0, tiled=True).reshape(chips * part, pair)

    away = picker(1 - core, part)
    came, came_t = joined([between_cores(away_columns(hidden, away, n, CHUNKS)) for n in range(CHUNKS)])
    keep, keep_t = kept_columns(hidden, picker(core, part))

    offset = lax.axis_index(ALL) * rows
    position = offset + jnp.arange(rows, dtype=jnp.int32)
    ends = jnp.cumsum(lengths)
    start = jnp.max(jnp.where(ends[None, :] <= position[:, None], ends[None, :], 0), axis=1)
    low = (start - (offset - SPAN * rows)).astype(jnp.int32)
    low = jnp.broadcast_to(low[:, None], (rows, pair // 2))

    partner = between_cores(mm(came, weight))
    key_value = (mm(keep, weight) + partner).astype(BF)
    pieces = window_pieces(key_value, core)

    attended, query_grad, swap, rest = attention(low, queries, out_grad, pieces)
    mine, other = returned(swap, rest, core)
    share = chip_share(keep_t, came_t, mine, other).reshape(chips, part, pair)
    spread = lax.all_to_all(share, CHIPS, 0, 0, tiled=True)
    return attended, query_grad, jnp.sum(spread.astype(F32), axis=0)


def solution(mesh):
    cuts, dp = mesh.devices.shape
    fine = Mesh(mesh.devices.reshape(cuts, 4, dp // 8, 2), ALL)
    rows = P(ALL, None)
    return jax.shard_map(
        per_device,
        mesh=fine,
        in_specs=(rows, rows, rows, rows, P()),
        out_specs=(rows, rows, rows),
        check_vma=False,
    )
```

profile of v0, /device:TPU:0, one launch (start us, length us, event | category | flops | bytes accessed | tf_op | source)
XLA Modules:
  0.0 162.6 jit_solution(14203119187172995930)
XLA Ops:
  0.6 2.4 %broadcast_in_dim.20 = bf16[64,64,256]{2,1,0:T(8,128)(2,1)} broadcast(bf16[64,256]{1,0:T(8,128)(2,1)} %param.6), dimensions={1,2} | broadcast | bytes 2129920 | tf_op jit(solution)/shard_map/broadcast_in_dim | solution.py:306
  3.0 11.5 %all-to-all-start = ((bf16[64,64,256]{2,1,0:T(8,128)(2,1)}), bf16[64,64,256]{2,1,0:T(8,128)(2,1)S(1)}, u32[]{:S(2)}, u32[]{:S(2)}) async-start(bf16[64,64,256]{2,1,0:T(8,128)(2,1)} %broadcast_in_dim.20), calls=%async_computation | async-start | bytes 4194304 | tf_op jit(solution)/shard_map/all_to_all | solution.py:307
  14.5 0.7 fusion.12.pick_ref
  15.2 2.6 %away_columns.4 = bf16[384,1024]{1,0:T(8,128)(2,1)} custom-call(bf16[256,128]{1,0:T(8,128)(2,1)} %fusion.12.pick_ref, bf16[384,8192]{1,0:T(8,128)(2,1)} %x_ref.9), custom_call_target="tpu_custom_call" | custom-call | bytes 2359296 | tf_op jit(solution)/shard_map/away_columns/pallas_call | solution.py:67
  17.8 0.0 collective-permute-start
  17.8 2.7 %away_columns.5 = bf16[384,1024]{1,0:T(8,128)(2,1)} custom-call(bf16[256,128]{1,0:T(8,128)(2,1)} %fusion.12.pick_ref, bf16[384,8192]{1,0:T(8,128)(2,1)} %x_ref.9), custom_call_target="tpu_custom_call" | custom-call | bytes 2359296 | tf_op jit(solution)/shard_map/away_columns/pallas_call | solution.py:67
  20.5 0.5 collective-permute-start.1
  20.9 2.7 %away_columns.6 = bf16[384,1024]{1,0:T(8,128)(2,1)} custom-call(bf16[256,128]{1,0:T(8,128)(2,1)} %fusion.12.pick_ref, bf16[384,8192]{1,0:T(8,128)(2,1)} %x_ref.9), custom_call_target="tpu_custom_call" | custom-call | bytes 2359296 | tf_op jit(solution)/shard_map/away_columns/pallas_call | solution.py:67
  23.6 0.0 collective-permute-start.2
  23.7 2.7 %away_columns.7 = bf16[384,1024]{1,0:T(8,128)(2,1)} custom-call(bf16[256,128]{1,0:T(8,128)(2,1)} %fusion.12.pick_ref, bf16[384,8192]{1,0:T(8,128)(2,1)} %x_ref.9), custom_call_target="tpu_custom_call" | custom-call | bytes 2359296 | tf_op jit(solution)/shard_map/away_columns/pallas_call | solution.py:67
  26.3 0.5 collective-permute-start.3
  26.8 0.7 fusion.11.pick_ref
  27.5 8.8 %kept_columns.1 = (bf16[384,4096]{1,0:T(8,128)(2,1)}, bf16[4096,384]{1,0:T(8,128)(2,1)}) custom-call(bf16[256,128]{1,0:T(8,128)(2,1)} %fusion.11.pick_ref, bf16[384,8192]{1,0:T(8,128)(2,1)} %x_ref.9), custom_call_target="tpu_custom_call" | custom-call | bytes 18874368 | tf_op jit(solution)/shard_map/kept_columns/pallas_call | solution.py:85
  36.3 0.0 copy-done.6
  36.3 0.3 reduce-window.9
  36.6 0.1 slice.25
  36.7 0.1 slice_reduce_fusion
  36.8 0.1 add_bitcast_fusion
  36.9 0.0 collective-permute-done.refs_0_
  36.9 0.0 collective-permute-done.1.refs_1_
  36.9 0.0 collective-permute-done.2.refs_2_
  36.9 0.0 collective-permute-done.3.refs_3_
  36.9 0.9 copy-done
  37.8 5.6 %joined.1 = (bf16[384,4096]{1,0:T(8,128)(2,1)}, bf16[4096,384]{1,0:T(8,128)(2,1)}) custom-call(bf16[384,1024]{1,0:T(8,128)(2,1)} %copy-done, bf16[384,1024]{1,0:T(8,128)(2,1)} %collective-permute-done.1.refs_1_, bf16[384,1024]{1,0:T(8,128)(2,1)} %collective-permute-done.2.refs_2_, bf16[384,1024]{1,0:T(8,128)(2,1)} %collective-permute-done.3.refs_3_), custom_call_target="tpu_custom_call" | custom-call | bytes 12582912 | tf_op jit(solution)/shard_map/joined/pallas_call | solution.py:105
  43.4 0.7 all-to-all-done
  44.1 3.0 %fusion.15 = f32[384,256]{1,0:T(8,128)S(1)} fusion(bf16[384,4096]{1,0:T(8,128)(2,1)} %get-tuple-element.12, bf16[4096,256]{1,0:T(8,128)(2,1)S(1)} %bitcast.24), kind=kOutput, calls=%fused_computation.37 | convolution fusion | flops 805306368 | bytes 5636096 | tf_op jit(solution)/shard_map/dot_general | solution.py:23
  47.1 0.1 collective-permute-start.4
  47.2 0.0 copy-done.7
  47.2 1.0 fusion.14
  48.2 0.7 collective-permute-done.4
  48.9 0.1 add_convert_fusion.refs_4_
  49.0 0.0 copy-start.1
  49.0 4.3 %collective-permute-start.5 = (bf16[384,256]{1,0:T(8,128)(2,1)S(1)}, bf16[384,256]{1,0:T(8,128)(2,1)S(1)}, u32[]{:S(2)}, u32[]{:S(2)}) collective-permute-start(bf16[384,256]{1,0:T(8,128)(2,1)S(1)} %add_convert_fusion.refs_4_), channel_id=1, source_target_pairs={{0,4},{1,5},{2,6},{3,7},{4,8},{5,9},{6,10},{7,11},{8,12},{9,13},{1... | collective-permute-start | bytes 589832 | tf_op jit(solution)/shard_map/ppermute | solution.py:278
  53.3 2.5 %collective-permute-start.6 = (bf16[384,256]{1,0:T(8,128)(2,1)S(1)}, bf16[384,256]{1,0:T(8,128)(2,1)S(1)}, u32[]{:S(2)}, u32[]{:S(2)}) collective-permute-start(bf16[384,256]{1,0:T(8,128)(2,1)S(1)} %add_convert_fusion.refs_4_), channel_id=1, source_target_pairs={{0,2},{1,3},{2,4},{3,5},{4,6},{5,7},{6,8},{7,9},{8,10},{9,11},{10,... | collective-permute-start | bytes 589832 | tf_op jit(solution)/shard_map/ppermute | solution.py:278
  55.8 0.1 select_reduce_fusion
  55.9 2.6 %collective-permute-done.5.refs_0_ = bf16[384,256]{1,0:T(8,128)(2,1)S(1)} collective-permute-done((bf16[384,256]{1,0:T(8,128)(2,1)S(1)}, bf16[384,256]{1,0:T(8,128)(2,1)S(1)}, u32[]{:S(2)}, u32[]{:S(2)}) %collective-permute-start.5) | collective-permute-done | bytes 196640 | tf_op jit(solution)/shard_map/ppermute | solution.py:278
  58.6 3.4 %collective-permute-done.6.refs_2_ = bf16[384,256]{1,0:T(8,128)(2,1)S(1)} collective-permute-done((bf16[384,256]{1,0:T(8,128)(2,1)S(1)}, bf16[384,256]{1,0:T(8,128)(2,1)S(1)}, u32[]{:S(2)}, u32[]{:S(2)}) %collective-permute-start.6) | collective-permute-done | bytes 196640 | tf_op jit(solution)/shard_map/ppermute | solution.py:278
  62.0 0.1 collective-permute-start.7
  62.1 0.5 collective-permute-start.8
  62.6 0.9 collective-permute-done.7.refs_1_
  63.5 0.3 collective-permute-done.8.refs_3_
  63.8 0.8 broadcast_in_dim.19.low_ref
  64.6 0.0 copy-done.1
  64.6 0.0 copy-done.3
  64.6 0.0 copy-done.4
  64.6 0.0 copy-done.8
  64.6 0.0 copy-done.9
  64.6 25.4 %attention.1 = (bf16[384,1024]{1,0:T(8,128)(2,1)}, bf16[384,1024]{1,0:T(8,128)(2,1)}, bf16[2,384,256]{2,1,0:T(8,128)(2,1)}, bf16[3,384,256]{2,1,0:T(8,128)(2,1)}) custom-call(s32[384,128]{1,0:T(8,128)} %broadcast_in_dim.19.low_ref, bf16[384,1024]{1,0:T(8,128)(2,1)} %q_ref.1, bf16[384,1024]{1,0:T(8,128)(2,1)} %g_ref.1, bf16[384,256]{1,0:T(8,128)(2,1)} %copy-done.3, ...), custom_call_target="tpu_custom_call" | custom-call | flops 18119393280 | bytes 3932160 | tf_op jit(solution)/shard_map/attention/pallas_call | solution.py:239
  90.1 0.3 collective-permute-start.9
  90.4 1.7 %collective-permute-done.9 = bf16[2,384,256]{2,1,0:T(8,128)(2,1)S(1)} collective-permute-done((bf16[2,384,256]{2,1,0:T(8,128)(2,1)}, bf16[2,384,256]{2,1,0:T(8,128)(2,1)S(1)}, u32[]{:S(2)}, u32[]{:S(2)}) %collective-permute-start.9) | collective-permute-done | bytes 393248 | tf_op jit(solution)/shard_map/ppermute | solution.py:272
  92.1 1.1 fusion.10
  93.2 1.3 collective-permute-start.10
  94.5 1.3 collective-permute-start.11
  95.8 7.1 %collective-permute-done.10 = bf16[384,256]{1,0:T(8,128)(2,1)S(1)} collective-permute-done((bf16[384,256]{1,0:T(8,128)(2,1)S(1)}, bf16[384,256]{1,0:T(8,128)(2,1)S(1)}, u32[]{:S(2)}, u32[]{:S(2)}) %collective-permute-start.10) | collective-permute-done | bytes 196640 | tf_op jit(solution)/shard_map/ppermute | solution.py:278
  102.9 3.7 %collective-permute-done.11 = bf16[384,256]{1,0:T(8,128)(2,1)S(1)} collective-permute-done((bf16[384,256]{1,0:T(8,128)(2,1)S(1)}, bf16[384,256]{1,0:T(8,128)(2,1)S(1)}, u32[]{:S(2)}, u32[]{:S(2)}) %collective-permute-start.11) | collective-permute-done | bytes 196640 | tf_op jit(solution)/shard_map/ppermute | solution.py:278
  106.6 1.1 fusion.4.mine_ref
  107.7 0.0 copy-start.2
  107.7 0.1 collective-permute-start.12
  107.8 1.4 collective-permute-done.12.other_ref
  109.2 0.0 copy-done.2
  109.2 0.7 copy-done.5
  109.9 8.1 %chip_share.1 = bf16[4096,256]{1,0:T(8,128)(2,1)} custom-call(bf16[4096,384]{1,0:T(8,128)(2,1)} %get-tuple-element.15.keep_ref, bf16[4096,384]{1,0:T(8,128)(2,1)} %get-tuple-element.16.came_ref, bf16[384,256]{1,0:T(8,128)(2,1)} %copy-done.2, bf16[384,256]{1,0:T(8,128)(2,1)} %copy-done.5), custom_call_target="tpu_custom_call" | custom-call | flops 1610612736 | bytes 9437184 | tf_op jit(solution)/shard_map/chip_share/pallas_call | solution.py:118
  117.9 43.7 %all_to_all.10 = bf16[64,64,256]{2,1,0:T(8,128)(2,1)S(1)} all-to-all(bf16[64,64,256]{2,1,0:T(8,128)(2,1)} %bitcast.23), channel_id=1, replica_groups=mesh['z'=4,'x'=4,'y'=4,'core'=2] {'z','x','y'}, dimensions={0} | all-to-all | bytes 4194304 | tf_op jit(solution)/shard_map/all_to_all | solution.py:327
  161.6 0.9 convert_reduce_fusion
  (15 shorter events, 0.1 us)
Async XLA Ops:
  3.0 41.1 %all-to-all-start = ((bf16[64,64,256]{2,1,0:T(8,128)(2,1)}), bf16[64,64,256]{2,1,0:T(8,128)(2,1)S(1)}, u32[]{:S(2)}, u32[]{:S(2)}) async-start(bf16[64,64,256]{2,1,0:T(8,128)(2,1)} %broadcast_in_dim.20), calls=%async_computation | async-start | bytes 4194304 | tf_op jit(solution)/shard_map/all_to_all | solution.py:307
  17.8 19.1 %collective-permute-start = (bf16[384,1024]{1,0:T(8,128)(2,1)}, bf16[384,1024]{1,0:T(8,128)(2,1)S(1)}, u32[]{:S(2)}, u32[]{:S(2)}) collective-permute-start(bf16[384,1024]{1,0:T(8,128)(2,1)} %away_columns.4), channel_id=1, source_target_pairs={{0,1},{1,0},{2,3},{3,2},{4,5},{5,4},{6,7},{7,6},{8,9},{9,8},{10,11... | collective-permute-start | bytes 2359304 | tf_op jit(solution)/shard_map/ppermute | solution.py:272
  20.5 16.4 %collective-permute-start.1 = (bf16[384,1024]{1,0:T(8,128)(2,1)}, bf16[384,1024]{1,0:T(8,128)(2,1)}, u32[]{:S(2)}, u32[]{:S(2)}) collective-permute-start(bf16[384,1024]{1,0:T(8,128)(2,1)} %away_columns.5), channel_id=1, source_target_pairs={{0,1},{1,0},{2,3},{3,2},{4,5},{5,4},{6,7},{7,6},{8,9},{9,8},{10,11... | collective-permute-start | bytes 2359304 | tf_op jit(solution)/shard_map/ppermute | solution.py:272
  23.6 13.3 %collective-permute-start.2 = (bf16[384,1024]{1,0:T(8,128)(2,1)}, bf16[384,1024]{1,0:T(8,128)(2,1)}, u32[]{:S(2)}, u32[]{:S(2)}) collective-permute-start(bf16[384,1024]{1,0:T(8,128)(2,1)} %away_columns.6), channel_id=1, source_target_pairs={{0,1},{1,0},{2,3},{3,2},{4,5},{5,4},{6,7},{7,6},{8,9},{9,8},{10,11... | collective-permute-start | bytes 2359304 | tf_op jit(solution)/shard_map/ppermute | solution.py:272
  26.3 10.6 %collective-permute-start.3 = (bf16[384,1024]{1,0:T(8,128)(2,1)}, bf16[384,1024]{1,0:T(8,128)(2,1)}, u32[]{:S(2)}, u32[]{:S(2)}) collective-permute-start(bf16[384,1024]{1,0:T(8,128)(2,1)} %away_columns.7), channel_id=1, source_target_pairs={{0,1},{1,0},{2,3},{3,2},{4,5},{5,4},{6,7},{7,6},{8,9},{9,8},{10,11... | collective-permute-start | bytes 2359304 | tf_op jit(solution)/shard_map/ppermute | solution.py:272
  27.5 8.8 %copy-start.6 = (s32[264]{0:T(512)S(1)}, s32[264]{0:T(512)}, u32[]{:S(2)}) copy-start(s32[264]{0:T(512)} %param.9) | copy-start | bytes 3172
  36.9 0.9 copy-start
  44.1 3.1 %copy-start.7 = (bf16[384,4096]{1,0:T(8,128)(2,1)S(1)}, bf16[384,4096]{1,0:T(8,128)(2,1)}, u32[]{:S(2)}) copy-start(bf16[384,4096]{1,0:T(8,128)(2,1)} %get-tuple-element.11) | copy-start | bytes 9437188
  47.1 1.8 %collective-permute-start.4 = (f32[384,256]{1,0:T(8,128)S(1)}, f32[384,256]{1,0:T(8,128)S(1)}, u32[]{:S(2)}, u32[]{:S(2)}) collective-permute-start(f32[384,256]{1,0:T(8,128)S(1)} %fusion.15), channel_id=1, source_target_pairs={{0,1},{1,0},{2,3},{3,2},{4,5},{5,4},{6,7},{7,6},{8,9},{9,8},{10,11... | collective-permute-start | bytes 1179656 | tf_op jit(solution)/shard_map/ppermute | solution.py:272
  49.0 15.6 %copy-start.1 = (bf16[384,256]{1,0:T(8,128)(2,1)}, bf16[384,256]{1,0:T(8,128)(2,1)S(1)}, u32[]{:S(2)}) copy-start(bf16[384,256]{1,0:T(8,128)(2,1)S(1)} %add_convert_fusion.refs_4_) | copy-start | bytes 589828
  49.0 9.6 %collective-permute-start.5 = (bf16[384,256]{1,0:T(8,128)(2,1)S(1)}, bf16[384,256]{1,0:T(8,128)(2,1)S(1)}, u32[]{:S(2)}, u32[]{:S(2)}) collective-permute-start(bf16[384,256]{1,0:T(8,128)(2,1)S(1)} %add_convert_fusion.refs_4_), channel_id=1, source_target_pairs={{0,4},{1,5},{2,6},{3,7},{4,8},{5,9},{6,10},{7,11},{8,12},{9,13},{1... | collective-permute-start | bytes 589832 | tf_op jit(solution)/shard_map/ppermute | solution.py:278
  53.3 8.7 %collective-permute-start.6 = (bf16[384,256]{1,0:T(8,128)(2,1)S(1)}, bf16[384,256]{1,0:T(8,128)(2,1)S(1)}, u32[]{:S(2)}, u32[]{:S(2)}) collective-permute-start(bf16[384,256]{1,0:T(8,128)(2,1)S(1)} %add_convert_fusion.refs_4_), channel_id=1, source_target_pairs={{0,2},{1,3},{2,4},{3,5},{4,6},{5,7},{6,8},{7,9},{8,10},{9,11},{10,... | collective-permute-start | bytes 589832 | tf_op jit(solution)/shard_map/ppermute | solution.py:278
  58.6 6.0 %copy-start.3 = (bf16[384,256]{1,0:T(8,128)(2,1)}, bf16[384,256]{1,0:T(8,128)(2,1)S(1)}, u32[]{:S(2)}) copy-start(bf16[384,256]{1,0:T(8,128)(2,1)S(1)} %collective-permute-done.5.refs_0_) | copy-start | bytes 589828
  62.0 2.6 %copy-start.4 = (bf16[384,256]{1,0:T(8,128)(2,1)}, bf16[384,256]{1,0:T(8,128)(2,1)S(1)}, u32[]{:S(2)}) copy-start(bf16[384,256]{1,0:T(8,128)(2,1)S(1)} %collective-permute-done.6.refs_2_) | copy-start | bytes 589828
  62.0 1.5 collective-permute-start.7
  62.1 1.7 %collective-permute-start.8 = (bf16[384,256]{1,0:T(8,128)(2,1)S(1)}, bf16[384,256]{1,0:T(8,128)(2,1)S(1)}, u32[]{:S(2)}, u32[]{:S(2)}) collective-permute-start(bf16[384,256]{1,0:T(8,128)(2,1)S(1)} %get-tuple-element.21), channel_id=1, source_target_pairs={{0,1},{1,0},{2,3},{3,2},{4,5},{5,4},{6,7},{7,6},{8,9},{9,8},{10,11... | collective-permute-start | bytes 589832 | tf_op jit(solution)/shard_map/ppermute | solution.py:272
  63.5 1.1 copy-start.8
  63.8 0.8 copy-start.9
  90.1 2.0 %collective-permute-start.9 = (bf16[2,384,256]{2,1,0:T(8,128)(2,1)}, bf16[2,384,256]{2,1,0:T(8,128)(2,1)S(1)}, u32[]{:S(2)}, u32[]{:S(2)}) collective-permute-start(bf16[2,384,256]{2,1,0:T(8,128)(2,1)} %get-tuple-element.18), channel_id=1, source_target_pairs={{0,1},{1,0},{2,3},{3,2},{4,5},{5,4},{6,7},{7,6},{8,9},{9,8},{10,11... | collective-permute-start | bytes 1179656 | tf_op jit(solution)/shard_map/ppermute | solution.py:272
  93.2 9.7 %collective-permute-start.10 = (bf16[384,256]{1,0:T(8,128)(2,1)S(1)}, bf16[384,256]{1,0:T(8,128)(2,1)S(1)}, u32[]{:S(2)}, u32[]{:S(2)}) collective-permute-start(bf16[384,256]{1,0:T(8,128)(2,1)S(1)} %get-tuple-element.19), channel_id=1, source_target_pairs={{2,0},{3,1},{4,2},{5,3},{6,4},{7,5},{8,6},{9,7},{10,8},{11,9},{12,... | collective-permute-start | bytes 589832 | tf_op jit(solution)/shard_map/ppermute | solution.py:278
  94.5 12.1 %collective-permute-start.11 = (bf16[384,256]{1,0:T(8,128)(2,1)S(1)}, bf16[384,256]{1,0:T(8,128)(2,1)S(1)}, u32[]{:S(2)}, u32[]{:S(2)}) collective-permute-start(bf16[384,256]{1,0:T(8,128)(2,1)S(1)} %get-tuple-element.20), channel_id=1, source_target_pairs={{4,0},{5,1},{6,2},{7,3},{8,4},{9,5},{10,6},{11,7},{12,8},{13,9},{1... | collective-permute-start | bytes 589832 | tf_op jit(solution)/shard_map/ppermute | solution.py:278
  107.7 1.5 copy-start.2
  107.7 1.5 collective-permute-start.12
  109.2 0.7 copy-start.5
where the time goes:
time: 164 us; the launch traced here: 163 us
  Pallas kernels  58.5 us (36%)
  blocking collectives  43.7 us (27%)
  starting transfers between devices  22.9 us (14%)
  waiting for transfers between devices  22.6 us (14%)
  other arithmetic  5.1 us (3%)
  local copies, waits for them, and re-layouts  4.89 us (3%)
  matrix products  4 us (2%)
    all_to_all x1, blocking collectives, per_device(): spread = lax.all_to_all(share, CHIPS, 0, 0, tiled=True)  43.7 us
    pallas_call x1, Pallas kernels, attention(): pl.pallas_call(attention_kernel, grid=(heads // HEADS_PER_STEP,), in_spec...  25.4 us
    ppermute x4, waiting for transfers between devices, between_chips(): return lax.ppermute(block, ALL, route)  16.8 us
    all_to_all x1, starting transfers between devices, per_device(): lax.all_to_all(copies, CHIPS, 0, 0, tiled=True).reshape(chips * part, pair)  11.5 us
    pallas_call x4, Pallas kernels, away_columns(): pl.pallas_call(away_kernel, grid=(2,), in_specs=[pl.BlockSpec((256, 128),...  10.7 us
    ppermute x4, starting transfers between devices, between_chips(): return lax.ppermute(block, ALL, route)  9.37 us
    pallas_call x1, Pallas kernels, kept_columns(): pl.pallas_call(keep_kernel, grid=(width // block,), in_specs=[pl.BlockSpe...  8.76 us
    pallas_call x1, Pallas kernels, chip_share(): pl.pallas_call(share_kernel, grid=(height // block,), in_specs=[pl.BlockS...  8.06 us
  transfers between devices with their start and end apart: 14, of which 10 were waited for; matrix products, arithmetic and copies ran while one was open for 2% of the time, Pallas kernels for 15%

commit v1 on v0

v1 whole, which is shorter than its diff:
```python
import functools
import math

import jax
import jax.numpy as jnp
from jax import lax
from jax.experimental import pallas as pl
from jax.experimental.pallas import tpu as pltpu
from jax.sharding import Mesh, PartitionSpec as P

SPAN = 4
PIECES = 6
NEG = -1e30
CHIPS = ("z", "x", "y")
ALL = ("z", "x", "y", "core")
SWAP = [(0, 1), (1, 0)]
CHUNKS = 4
BF = jnp.bfloat16
F32 = jnp.float32


def mm(a, b):
    return jnp.dot(a, b, preferred_element_type=F32)


def pick_kernel(pick_ref, x_ref, out_ref):
    for n in range(x_ref.shape[1] // 256):
        y = mm(x_ref[:, n * 256 : (n + 1) * 256], pick_ref[...])
        out_ref[:, n * 128 : (n + 1) * 128] = y.astype(BF)


def across(a, b):
    return lax.dot_general(a, b, (((0,), (0,)), ((), ())), preferred_element_type=F32)


def share_kernel(*refs):
    chunks = (len(refs) - 3) // 2
    mine_ref, other_ref, share_ref = refs[-3:]
    for n in range(chunks):
        both = across(refs[n][...], mine_ref[...]) + across(refs[chunks + n][...], other_ref[...])
        share_ref[n] = both.astype(BF)


def project_kernel(*refs):
    parts, (weight_ref, out_ref) = refs[:-2], refs[-2:]
    width = parts[0].shape[1]
    out_ref[...] = sum(mm(part[...], weight_ref[n * width : (n + 1) * width, :]) for n, part in enumerate(parts))


def params(mib=56):
    return pltpu.CompilerParams(vmem_limit_bytes=mib * 1024 * 1024)


def picker(side, part):
    out = jnp.arange(128, dtype=jnp.int32)
    source = (out // part) * 2 * part + side * part + out % part
    return (jnp.arange(256, dtype=jnp.int32)[:, None] == source[None, :]).astype(BF)


def picked_columns(hidden, pick, chunk, chunks):
    rows, width = hidden.shape
    block = 1024
    steps = width // (block * chunks)
    return pl.pallas_call(
        pick_kernel,
        grid=(steps,),
        in_specs=[
            pl.BlockSpec((256, 128), lambda i: (0, 0)),
            pl.BlockSpec((rows, block), lambda i: (0, steps * chunk + i)),
        ],
        out_specs=pl.BlockSpec((rows, block // 2), lambda i: (0, i)),
        out_shape=jax.ShapeDtypeStruct((rows, steps * block // 2), BF),
        cost_estimate=pl.CostEstimate(flops=0, bytes_accessed=3 * rows * block * steps, transcendentals=0),
        compiler_params=params(),
        name="picked_columns",
    )(pick, hidden)


def chip_share(keep, came, mine, other):
    rows, width = keep.shape
    pair = mine.shape[1]
    chunks = len(came)
    block = width // (2 * chunks)
    whole = pl.BlockSpec((rows, pair), lambda i: (0, 0))
    return pl.pallas_call(
        share_kernel,
        grid=(2,),
        in_specs=[pl.BlockSpec((rows, block), lambda i, n=n: (0, 2 * n + i)) for n in range(chunks)]
        + [pl.BlockSpec((rows, block), lambda i: (0, i))] * chunks
        + [whole, whole],
        out_specs=pl.BlockSpec((chunks, block, pair), lambda i: (0, i, 0)),
        out_shape=jax.ShapeDtypeStruct((chunks, 2 * block, pair), BF),
        cost_estimate=pl.CostEstimate(flops=4 * width * rows * pair, bytes_accessed=6 * width * rows, transcendentals=0),
        compiler_params=params(),
        name="chip_share",
    )(*([keep] * chunks), *came, mine, other)


def projected(came, weight):
    rows, pair = came[0].shape[0], weight.shape[1]
    return pl.pallas_call(
        project_kernel,
        out_shape=jax.ShapeDtypeStruct((rows, pair), F32),
        cost_estimate=pl.CostEstimate(flops=2 * rows * weight.size, bytes_accessed=2 * weight.size, transcendentals=0),
        compiler_params=params(16),
        name="projected",
    )(*came, weight)


def key_chunks(rows):
    edge, span = 2 * rows // 3, (SPAN + 1) * rows
    chunks = [(0, edge, 0, edge)]
    at = edge
    while at < span - edge:
        end = min(at + 768, span - edge)
        chunks.append((at, end, 0, rows))
        at = end
    chunks.append((span - edge, span, rows - edge, rows))
    return chunks


def onto_rows(total, extra, first, end):
    parts = [total[:first], total[first:end] + extra, total[end:]]
    return jnp.concatenate([part for part in parts if part.shape[0]], axis=0)


def lane_groups(block, size):
    return [block[:, n : n + size] for n in range(0, block.shape[1], size)]


def attention_kernel(place_ref, ends_ref, q_ref, g_ref, *refs):
    pieces = refs[:PIECES]
    out_ref, dq_ref, swap_ref, rest_ref, kv_ref, turned_ref, bias_ref, s_ref, p_ref, acc_ref = refs[PIECES:]
    step = pl.program_id(0)
    rows = q_ref.shape[0]
    size = kv_ref.shape[1] // 2
    span = kv_ref.shape[0]
    chunks = key_chunks(rows)
    scale = 1.0 / math.sqrt(size)
    scale2 = scale * math.log2(math.e)

    @pl.when(step == 0)
    def _():
        offset, core, ends = place_ref[0], place_ref[1], ends_ref[...]
        position = offset + lax.broadcasted_iota(jnp.int32, (rows, ends.shape[1]), 0)
        start = jnp.max(jnp.where(ends <= position, ends, 0), axis=1, keepdims=True)
        low = start - (offset - SPAN * rows)
        row = lax.broadcasted_iota(jnp.int32, (rows, rows), 0)
        own, second, fourth, other_own, other_second, other_fourth = [piece[...] for piece in pieces]
        first = jnp.where(core == 0, other_second, other_own)
        third = jnp.where(core == 0, other_fourth, other_second)
        for j, piece in enumerate([fourth, third, second, first, own]):
            cols = slice(j * rows, (j + 1) * rows)
            kv_ref[cols, :] = piece
            turned_ref[:size, cols] = piece[:, :size].T
            turned_ref[size:, cols] = piece[:, size:].T
            at = lax.broadcasted_iota(jnp.int32, (rows, rows), 1) + j * rows
            allowed = (at >= low) & (at <= row + SPAN * rows)
            bias_ref[:, cols] = jnp.where(allowed, 0.0, NEG)
        acc_ref[...] = jnp.zeros_like(acc_ref)

    def one_head(h):
        lanes = slice(h * size, (h + 1) * size)
        q = q_ref[:, lanes]
        top = jnp.full((rows, size), NEG, F32)
        for c0, c1, r0, r1 in chunks:
            s = mm(q[r0:r1], turned_ref[:size, c0:c1]) + bias_ref[r0:r1, c0:c1]
            s_ref[h % 2, r0:r1, c0:c1] = s
            most = functools.reduce(jnp.maximum, lane_groups(s, size))
            parts = [top[:r0], jnp.maximum(top[r0:r1], most), top[r1:]]
            top = jnp.concatenate([part for part in parts if part.shape[0]], axis=0)
            yield
        peak = jnp.max(top, axis=1, keepdims=True) * scale2
        total = jnp.zeros((rows, size), F32)
        out = jnp.zeros((rows, size), F32)
        for c0, c1, r0, r1 in chunks:
            e = jnp.exp2(s_ref[h % 2, r0:r1, c0:c1] * scale2 - peak[r0:r1])
            total = onto_rows(total, functools.reduce(jnp.add, lane_groups(e, size)), r0, r1)
            p = e.astype(BF)
            p_ref[h % 2, r0:r1, c0:c1] = p
            out = onto_rows(out, mm(p, kv_ref[c0:c1, size:]), r0, r1)
            yield
        inverse = 1.0 / jnp.sum(total, axis=1, keepdims=True)
        out = out * inverse
        out_ref[:, lanes] = out.astype(BF)
        scaled = g_ref[:, lanes].astype(F32) * inverse
        g = scaled.astype(BF)
        delta = jnp.sum(g.astype(F32) * out, axis=1, keepdims=True)
        g_turned = scaled.T.astype(BF)
        q_turned = q.astype(F32).T.astype(BF)
        dq = jnp.zeros((rows, size), F32)
        for c0, c1, r0, r1 in chunks:
            p = p_ref[h % 2, r0:r1, c0:c1]
            acc_ref[size:, c0:c1] += mm(g_turned[:, r0:r1], p)
            dp = mm(g[r0:r1], turned_ref[size:, c0:c1]) - delta[r0:r1]
            ds = dp.astype(BF) * p
            dq = onto_rows(dq, mm(ds, kv_ref[c0:c1, :size]), r0, r1)
            acc_ref[:size, c0:c1] += mm(q_turned[:, r0:r1], ds)
            yield
        dq_ref[:, lanes] = (dq * scale).astype(BF)

    running, waiting = [], [one_head(h) for h in range(q_ref.shape[1] // size)]
    while running or waiting:
        if waiting:
            running.append(waiting.pop(0))
        for _ in chunks:
            running = [head for head in running if next(head, head) is None]

    @pl.when(step == pl.num_programs(0) - 1)
    def _():
        for j in range(SPAN + 1):
            cols = slice(j * rows, (j + 1) * rows)
            into = rest_ref.at[j // 2] if j % 2 == 0 else swap_ref.at[1 - j // 2]
            into[:, :size] = (acc_ref[:size, cols].T * scale).astype(BF)
            into[:, size:] = acc_ref[size:, cols].T.astype(BF)


HEADS_PER_STEP = 4


def attention(place, ends, queries, out_grad, pieces):
    rows, width = queries.shape
    pair = pieces[0].shape[1]
    size = pair // 2
    heads = width // size
    span = (SPAN + 1) * rows
    several = pl.BlockSpec((rows, HEADS_PER_STEP * size), lambda h: (0, h))
    whole = pl.BlockSpec((rows, pair), lambda h: (0, 0))
    return pl.pallas_call(
        attention_kernel,
        grid=(heads // HEADS_PER_STEP,),
        in_specs=[
            pl.BlockSpec(memory_space=pltpu.SMEM),
            pl.BlockSpec((1, ends.shape[1]), lambda h: (0, 0)),
            several,
            several,
        ]
        + [whole] * PIECES,
        out_specs=[
            several,
            several,
            pl.BlockSpec((SPAN // 2, rows, pair), lambda h: (0, 0, 0)),
            pl.BlockSpec((SPAN // 2 + 1, rows, pair), lambda h: (0, 0, 0)),
        ],
        out_shape=[
            jax.ShapeDtypeStruct((rows, width), BF),
            jax.ShapeDtypeStruct((rows, width), BF),
            jax.ShapeDtypeStruct((SPAN // 2, rows, pair), BF),
            jax.ShapeDtypeStruct((SPAN // 2 + 1, rows, pair), BF),
        ],
        scratch_shapes=[
            pltpu.VMEM((span, pair), BF),
            pltpu.VMEM((pair, span), BF),
            pltpu.VMEM((rows, span), F32),
            pltpu.VMEM((2, rows, span), F32),
            pltpu.VMEM((2, rows, span), BF),
            pltpu.VMEM((pair, span), F32),
        ],
        cost_estimate=pl.CostEstimate(
            flops=24 * heads * rows * span * size, bytes_accessed=10 * rows * width, transcendentals=heads * rows * span
        ),
        compiler_params=params(56),
        name="attention",
    )(place, ends, queries, out_grad, *pieces)


def between_cores(block):
    return lax.ppermute(block, "core", SWAP)


def between_chips(block, distance):
    devices = range(lax.axis_size(ALL))
    route = [(i, i + 2 * distance) for i in devices if i + 2 * distance in devices]
    return lax.ppermute(block, ALL, route)


def window_pieces(key_value):
    second = between_chips(key_value, 1)
    fourth = between_chips(key_value, 2)
    mine = [key_value, second, fourth]
    return mine + [between_cores(block) for block in mine]


def returned(swap, rest, core):
    came = between_cores(swap)
    first, third = came[0].astype(F32), came[1].astype(F32)
    near = (rest[1].astype(F32) + jnp.where(core == 0, third, first)).astype(BF)
    far = (rest[0].astype(F32) + jnp.where(core == 0, 0.0, third)).astype(BF)
    own = rest[2].astype(F32) + jnp.where(core == 0, first, 0.0)
    summed = own + between_chips(near, -1).astype(F32) + between_chips(far, -2).astype(F32)
    mine = summed.astype(BF)
    return mine, between_cores(mine)


def per_device(hidden, kv_weight, queries, out_grad, lengths):
    rows = hidden.shape[0]
    part, pair = kv_weight.shape
    core = lax.axis_index("core")
    chips = lax.axis_size(CHIPS)

    copies = jnp.broadcast_to(kv_weight[None], (chips, part, pair))
    weight = lax.all_to_all(copies, CHIPS, 0, 0, tiled=True).reshape(chips * part, pair)

    away = picker(1 - core, part)
    came = [between_cores(picked_columns(hidden, away, n, CHUNKS)) for n in range(CHUNKS)]
    keep = picked_columns(hidden, picker(core, part), 0, 1)

    place = jnp.stack([lax.axis_index(ALL) * rows, core]).astype(jnp.int32)
    ends = jnp.cumsum(lengths).astype(jnp.int32)[None, :]

    place, ends, keep = lax.optimization_barrier((place, ends, keep))
    partner = between_cores(projected(came, weight))
    key_value = (mm(keep, weight) + partner).astype(BF)
    pieces = window_pieces(key_value)

    attended, query_grad, swap, rest = attention(place, ends, queries, out_grad, pieces)
    mine, other = returned(swap, rest, core)
    share = chip_share(keep, came, mine, other).reshape(chips, part, pair)
    spread = lax.all_to_all(share, CHIPS, 0, 0, tiled=True)
    return attended, query_grad, jnp.sum(spread.astype(F32), axis=0)


def solution(mesh):
    cuts, dp = mesh.devices.shape
    fine = Mesh(mesh.devices.reshape(cuts, 4, dp // 8, 2), ALL)
    rows = P(ALL, None)
    return jax.shard_map(
        per_device,
        mesh=fine,
        in_specs=(rows, rows, rows, rows, P()),
        out_specs=(rows, rows, rows),
        check_vma=False,
    )
```

time: 164 us -> 156 us (0.951)
  Pallas kernels: 58.5 us -> 50.8 us
  waiting for transfers between devices: 22.6 us -> 29.3 us
  matrix products: 4 us -> 1.01 us
    all_to_all x1, waiting for transfers between devices: 0.69 us -> 6.62 us  [per_device(): lax.all_to_all(copies, CHIPS, 0, 0, tiled=True).reshape(chips * part, pair)]
    pallas_call x7, Pallas kernels: 33.1 us -> 27.5 us  [the longest x5 18.8 us: picked_columns(): pl.pallas_call(pick_kernel, grid=(steps,), in_specs=[pl.BlockSpec((256, 1...]
    dot_general x2 -> x1, matrix products: 4 us -> 1.01 us  [mm(): return jnp.dot(a, b, preferred_element_type=F32)]
    pallas_call x1, Pallas kernels: 25.4 us -> 23.2 us  [attention(): pl.pallas_call(attention_kernel, grid=(heads // HEADS_PER_STEP,), in_spec...]
    ppermute x9 -> x10, waiting for transfers between devices: 5.06 us -> 5.34 us  [between_cores(): return lax.ppermute(block, 'core', SWAP)]
  transfers between devices with their start and end apart: 14 -> 15, of which waited for: 10 -> 9; matrix products, arithmetic and copies ran while one was open for 2% -> 3% of each run, Pallas kernels for 15% -> 12%
where the time goes in v1:
time: 156 us
  Pallas kernels  50.8 us (33%)
  blocking collectives  42.3 us (27%)
  waiting for transfers between devices  29.3 us (19%)
  starting transfers between devices  21.4 us (14%)
  other arithmetic  5.48 us (4%)
  local copies, waits for them, and re-layouts  4.55 us (3%)
    all_to_all x1, blocking collectives, per_device(): spread = lax.all_to_all(share, CHIPS, 0, 0, tiled=True)  42.3 us
    pallas_call x1, Pallas kernels, attention(): pl.pallas_call(attention_kernel, grid=(heads // HEADS_PER_STEP,), in_spec...  23.2 us
    pallas_call x5, Pallas kernels, picked_columns(): pl.pallas_call(pick_kernel, grid=(steps,), in_specs=[pl.BlockSpec((256, 1...  18.8 us
    ppermute x4, waiting for transfers between devices, between_chips(): return lax.ppermute(block, ALL, route)  17.4 us
    all_to_all x1, starting transfers between devices, per_device(): lax.all_to_all(copies, CHIPS, 0, 0, tiled=True).reshape(chips * part, pair)  11.5 us
    ppermute x4, starting transfers between devices, between_chips(): return lax.ppermute(block, ALL, route)  8.17 us
    all_to_all x1, waiting for transfers between devices, per_device(): lax.all_to_all(copies, CHIPS, 0, 0, tiled=True).reshape(chips * part, pair)  6.62 us
    pallas_call x1, Pallas kernels, chip_share(): pl.pallas_call(share_kernel, grid=(2,), in_specs=[pl.BlockSpec((rows, blo...  5.99 us
  transfers between devices with their start and end apart: 15, of which 9 were waited for; matrix products, arithmetic and copies ran while one was open for 3% of the time, Pallas kernels for 12%

profile of v1, /device:TPU:0, one launch (start us, length us, event | category | flops | bytes accessed | tf_op | source)
XLA Modules:
  0.0 155.6 jit_solution(16560422354101121448)
XLA Ops:
  0.6 2.4 %broadcast_in_dim.9 = bf16[64,64,256]{2,1,0:T(8,128)(2,1)} broadcast(bf16[64,256]{1,0:T(8,128)(2,1)} %param.6), dimensions={1,2} | broadcast | bytes 2129920 | tf_op jit(solution)/shard_map/broadcast_in_dim | solution.py:301
  3.0 11.5 %all-to-all-start = ((bf16[64,64,256]{2,1,0:T(8,128)(2,1)}), bf16[64,64,256]{2,1,0:T(8,128)(2,1)S(1)}, u32[]{:S(2)}, u32[]{:S(2)}) async-start(bf16[64,64,256]{2,1,0:T(8,128)(2,1)} %broadcast_in_dim.9), calls=%async_computation | async-start | bytes 4194304 | tf_op jit(solution)/shard_map/all_to_all | solution.py:302
  14.5 0.7 fusion.12.pick_ref
  15.2 2.6 %picked_columns.6 = bf16[384,1024]{1,0:T(8,128)(2,1)} custom-call(bf16[256,128]{1,0:T(8,128)(2,1)} %fusion.12.pick_ref, bf16[384,8192]{1,0:T(8,128)(2,1)} %x_ref.9), custom_call_target="tpu_custom_call" | custom-call | bytes 2359296 | tf_op jit(solution)/shard_map/picked_columns/pallas_call | solution.py:64
  17.8 0.0 collective-permute-start
  17.8 2.7 %picked_columns.7 = bf16[384,1024]{1,0:T(8,128)(2,1)} custom-call(bf16[256,128]{1,0:T(8,128)(2,1)} %fusion.12.pick_ref, bf16[384,8192]{1,0:T(8,128)(2,1)} %x_ref.9), custom_call_target="tpu_custom_call" | custom-call | bytes 2359296 | tf_op jit(solution)/shard_map/picked_columns/pallas_call | solution.py:64
  20.5 0.5 collective-permute-start.1
  21.0 2.7 %picked_columns.8 = bf16[384,1024]{1,0:T(8,128)(2,1)} custom-call(bf16[256,128]{1,0:T(8,128)(2,1)} %fusion.12.pick_ref, bf16[384,8192]{1,0:T(8,128)(2,1)} %x_ref.9), custom_call_target="tpu_custom_call" | custom-call | bytes 2359296 | tf_op jit(solution)/shard_map/picked_columns/pallas_call | solution.py:64
  23.7 0.0 collective-permute-start.2
  23.7 2.7 %picked_columns.9 = bf16[384,1024]{1,0:T(8,128)(2,1)} custom-call(bf16[256,128]{1,0:T(8,128)(2,1)} %fusion.12.pick_ref, bf16[384,8192]{1,0:T(8,128)(2,1)} %x_ref.9), custom_call_target="tpu_custom_call" | custom-call | bytes 2359296 | tf_op jit(solution)/shard_map/picked_columns/pallas_call | solution.py:64
  26.4 0.5 collective-permute-start.3
  26.8 0.0 copy-done.5
  26.9 0.3 reduce-window.9
  27.2 0.1 slice.25
  27.3 0.1 slice_reduce_fusion
  27.4 0.1 add_bitcast_fusion
  27.5 0.6 broadcast_in_dim.8.ends_ref
  28.1 0.7 fusion.11.pick_ref
  28.7 8.1 %picked_columns.5.refs_0_.refs_1_.refs_2_.refs_3_ = bf16[384,4096]{1,0:T(8,128)(2,1)} custom-call(bf16[256,128]{1,0:T(8,128)(2,1)} %fusion.11.pick_ref, bf16[384,8192]{1,0:T(8,128)(2,1)} %x_ref.9), custom_call_target="tpu_custom_call" | custom-call | bytes 9437184 | tf_op jit(solution)/shard_map/picked_columns/pallas_call | solution.py:64
  36.9 0.6 pad_add_fusion.place_ref
  37.5 0.0 collective-permute-done.refs_0_.refs_4_
  37.5 0.0 collective-permute-done.1.refs_1_.refs_5_
  37.5 0.0 collective-permute-done.2.refs_2_.refs_6_
  37.5 0.0 collective-permute-done.3.refs_3_.refs_7_
  37.5 6.6 %all-to-all-done = bf16[64,64,256]{2,1,0:T(8,128)(2,1)S(1)} async-done(((bf16[64,64,256]{2,1,0:T(8,128)(2,1)}), bf16[64,64,256]{2,1,0:T(8,128)(2,1)S(1)}, u32[]{:S(2)}, u32[]{:S(2)}) %all-to-all-start) | async-done | bytes 2097184 | tf_op jit(solution)/shard_map/all_to_all | solution.py:302
  44.1 2.7 %projected.1 = f32[384,256]{1,0:T(8,128)S(1)} custom-call(bf16[384,1024]{1,0:T(8,128)(2,1)S(1)} %collective-permute-done.refs_0_.refs_4_, bf16[384,1024]{1,0:T(8,128)(2,1)} %collective-permute-done.1.refs_1_.refs_5_, bf16[384,1024]{1,0:T(8,128)(2,1)} %collective-permute-done.2.refs_2_.refs_6_, bf16[384,1024]{1,0:T(8,128)(2,1)} %collective-permute-done.3.refs_3_.refs_7_, ...), custom_call_target="tpu_custom_call" | custom-call | flops 805306368 | bytes 2097152 | tf_op jit(solution)/shard_map/projected/pallas_call | solution.py:101
  46.8 0.0 copy-done
  46.9 0.1 collective-permute-start.4
  46.9 0.0 copy-done.1
  47.0 1.0 fusion.14
  48.0 0.7 collective-permute-done.4
  48.7 0.1 add_convert_fusion.refs_0_
  48.7 0.0 copy-start.4
  48.7 3.7 %collective-permute-start.6 = (bf16[384,256]{1,0:T(8,128)(2,1)S(1)}, bf16[384,256]{1,0:T(8,128)(2,1)S(1)}, u32[]{:S(2)}, u32[]{:S(2)}) collective-permute-start(bf16[384,256]{1,0:T(8,128)(2,1)S(1)} %add_convert_fusion.refs_0_), channel_id=1, source_target_pairs={{0,4},{1,5},{2,6},{3,7},{4,8},{5,9},{6,10},{7,11},{8,12},{9,13},{1... | collective-permute-start | bytes 589832 | tf_op jit(solution)/shard_map/ppermute | solution.py:274
  52.4 1.9 %collective-permute-start.5 = (bf16[384,256]{1,0:T(8,128)(2,1)S(1)}, bf16[384,256]{1,0:T(8,128)(2,1)S(1)}, u32[]{:S(2)}, u32[]{:S(2)}) collective-permute-start(bf16[384,256]{1,0:T(8,128)(2,1)S(1)} %add_convert_fusion.refs_0_), channel_id=1, source_target_pairs={{0,2},{1,3},{2,4},{3,5},{4,6},{5,7},{6,8},{7,9},{8,10},{9,11},{10,... | collective-permute-start | bytes 589832 | tf_op jit(solution)/shard_map/ppermute | solution.py:274
  54.3 0.1 collective-permute-start.7
  54.4 3.3 %collective-permute-done.6.refs_2_ = bf16[384,256]{1,0:T(8,128)(2,1)S(1)} collective-permute-done((bf16[384,256]{1,0:T(8,128)(2,1)S(1)}, bf16[384,256]{1,0:T(8,128)(2,1)S(1)}, u32[]{:S(2)}, u32[]{:S(2)}) %collective-permute-start.6) | collective-permute-done | bytes 196640 | tf_op jit(solution)/shard_map/ppermute | solution.py:274
  57.7 0.0 collective-permute-start.9
  57.7 3.4 %collective-permute-done.5.refs_1_ = bf16[384,256]{1,0:T(8,128)(2,1)S(1)} collective-permute-done((bf16[384,256]{1,0:T(8,128)(2,1)S(1)}, bf16[384,256]{1,0:T(8,128)(2,1)S(1)}, u32[]{:S(2)}, u32[]{:S(2)}) %collective-permute-start.5) | collective-permute-done | bytes 196640 | tf_op jit(solution)/shard_map/ppermute | solution.py:274
  61.1 0.0 collective-permute-start.8
  61.1 0.0 collective-permute-done.7.refs_3_
  61.1 0.0 copy-start.8
  61.1 0.0 collective-permute-done.9.refs_5_
  61.1 0.0 copy-start.9
  61.1 1.4 collective-permute-done.8.refs_4_
  62.5 0.0 copy-done.4
  62.5 0.0 copy-done.6
  62.6 0.7 copy-done.10
  63.2 23.2 %attention.1 = (bf16[384,1024]{1,0:T(8,128)(2,1)}, bf16[384,1024]{1,0:T(8,128)(2,1)}, bf16[2,384,256]{2,1,0:T(8,128)(2,1)}, bf16[3,384,256]{2,1,0:T(8,128)(2,1)}) custom-call(s32[2]{0:T(128)} %pad_add_fusion.place_ref, s32[1,264]{1,0:T(1,128)} %broadcast_in_dim.8.ends_ref, bf16[384,1024]{1,0:T(8,128)(2,1)} %q_ref.1, bf16[384,1024]{1,0:T(8,128)(2,1)} %g_ref.1, ...), custom_call_target="tpu_custom_call" | custom-call | flops 18119393280 | bytes 3932160 | tf_op jit(solution)/shard_map/attention/pallas_call | solution.py:229
  86.5 0.2 collective-permute-start.10
  86.7 1.8 %collective-permute-done.10 = bf16[2,384,256]{2,1,0:T(8,128)(2,1)S(1)} collective-permute-done((bf16[2,384,256]{2,1,0:T(8,128)(2,1)}, bf16[2,384,256]{2,1,0:T(8,128)(2,1)S(1)}, u32[]{:S(2)}, u32[]{:S(2)}) %collective-permute-start.10) | collective-permute-done | bytes 393248 | tf_op jit(solution)/shard_map/ppermute | solution.py:268
  88.5 1.1 fusion.10
  89.6 1.3 collective-permute-start.11
  90.9 1.3 collective-permute-start.12
  92.2 7.0 %collective-permute-done.11 = bf16[384,256]{1,0:T(8,128)(2,1)S(1)} collective-permute-done((bf16[384,256]{1,0:T(8,128)(2,1)S(1)}, bf16[384,256]{1,0:T(8,128)(2,1)S(1)}, u32[]{:S(2)}, u32[]{:S(2)}) %collective-permute-start.11) | collective-permute-done | bytes 196640 | tf_op jit(solution)/shard_map/ppermute | solution.py:274
  99.2 3.7 %collective-permute-done.12 = bf16[384,256]{1,0:T(8,128)(2,1)S(1)} collective-permute-done((bf16[384,256]{1,0:T(8,128)(2,1)S(1)}, bf16[384,256]{1,0:T(8,128)(2,1)S(1)}, u32[]{:S(2)}, u32[]{:S(2)}) %collective-permute-start.12) | collective-permute-done | bytes 196640 | tf_op jit(solution)/shard_map/ppermute | solution.py:274
  102.9 1.0 fusion.4.refs_8_
  104.0 0.0 copy-start.2
  104.0 0.3 collective-permute-start.13
  104.3 1.4 collective-permute-done.13.refs_9_
  105.7 0.7 copy-done.3
  106.4 6.0 %chip_share.1 = bf16[4,1024,256]{2,1,0:T(8,128)(2,1)} custom-call(bf16[384,4096]{1,0:T(8,128)(2,1)} %picked_columns.5.refs_0_.refs_1_.refs_2_.refs_3_, bf16[384,4096]{1,0:T(8,128)(2,1)} %picked_columns.5.refs_0_.refs_1_.refs_2_.refs_3_, bf16[384,4096]{1,0:T(8,128)(2,1)} %picked_columns.5.refs_0_.refs_1_.refs_2_.refs_3_, ...), custom_call_target="tpu_custom_call" | custom-call | flops 1610612736 | bytes 9437184 | tf_op jit(solution)/shard_map/chip_share/pallas_call | solution.py:85
  112.4 42.3 %all_to_all.10 = bf16[64,64,256]{2,1,0:T(8,128)(2,1)S(1)} all-to-all(bf16[64,64,256]{2,1,0:T(8,128)(2,1)} %bitcast.25), channel_id=1, replica_groups=mesh['z'=4,'x'=4,'y'=4,'core'=2] {'z','x','y'}, dimensions={0} | all-to-all | bytes 4194304 | tf_op jit(solution)/shard_map/all_to_all | solution.py:319
  154.7 0.9 convert_reduce_fusion
  (15 shorter events, 0.1 us)
Async XLA Ops:
  3.0 41.1 %all-to-all-start = ((bf16[64,64,256]{2,1,0:T(8,128)(2,1)}), bf16[64,64,256]{2,1,0:T(8,128)(2,1)S(1)}, u32[]{:S(2)}, u32[]{:S(2)}) async-start(bf16[64,64,256]{2,1,0:T(8,128)(2,1)} %broadcast_in_dim.9), calls=%async_computation | async-start | bytes 4194304 | tf_op jit(solution)/shard_map/all_to_all | solution.py:302
  17.8 19.6 %collective-permute-start = (bf16[384,1024]{1,0:T(8,128)(2,1)}, bf16[384,1024]{1,0:T(8,128)(2,1)S(1)}, u32[]{:S(2)}, u32[]{:S(2)}) collective-permute-start(bf16[384,1024]{1,0:T(8,128)(2,1)} %picked_columns.6), channel_id=1, source_target_pairs={{0,1},{1,0},{2,3},{3,2},{4,5},{5,4},{6,7},{7,6},{8,9},{9,8},{10,11... | collective-permute-start | bytes 2359304 | tf_op jit(solution)/shard_map/ppermute | solution.py:268
  20.5 17.0 %collective-permute-start.1 = (bf16[384,1024]{1,0:T(8,128)(2,1)}, bf16[384,1024]{1,0:T(8,128)(2,1)}, u32[]{:S(2)}, u32[]{:S(2)}) collective-permute-start(bf16[384,1024]{1,0:T(8,128)(2,1)} %picked_columns.7), channel_id=1, source_target_pairs={{0,1},{1,0},{2,3},{3,2},{4,5},{5,4},{6,7},{7,6},{8,9},{9,8},{10,11... | collective-permute-start | bytes 2359304 | tf_op jit(solution)/shard_map/ppermute | solution.py:268
  23.7 3.2 %copy-start.5 = (s32[264]{0:T(512)S(1)}, s32[264]{0:T(512)}, u32[]{:S(2)}) copy-start(s32[264]{0:T(512)} %param.9) | copy-start | bytes 3172
  23.7 13.8 %collective-permute-start.2 = (bf16[384,1024]{1,0:T(8,128)(2,1)}, bf16[384,1024]{1,0:T(8,128)(2,1)}, u32[]{:S(2)}, u32[]{:S(2)}) collective-permute-start(bf16[384,1024]{1,0:T(8,128)(2,1)} %picked_columns.8), channel_id=1, source_target_pairs={{0,1},{1,0},{2,3},{3,2},{4,5},{5,4},{6,7},{7,6},{8,9},{9,8},{10,11... | collective-permute-start | bytes 2359304 | tf_op jit(solution)/shard_map/ppermute | solution.py:268
  26.4 11.1 %collective-permute-start.3 = (bf16[384,1024]{1,0:T(8,128)(2,1)}, bf16[384,1024]{1,0:T(8,128)(2,1)}, u32[]{:S(2)}, u32[]{:S(2)}) collective-permute-start(bf16[384,1024]{1,0:T(8,128)(2,1)} %picked_columns.9), channel_id=1, source_target_pairs={{0,1},{1,0},{2,3},{3,2},{4,5},{5,4},{6,7},{7,6},{8,9},{9,8},{10,11... | collective-permute-start | bytes 2359304 | tf_op jit(solution)/shard_map/ppermute | solution.py:268
  37.5 9.4 %copy-start = (bf16[384,1024]{1,0:T(8,128)(2,1)}, bf16[384,1024]{1,0:T(8,128)(2,1)S(1)}, u32[]{:S(2)}) copy-start(bf16[384,1024]{1,0:T(8,128)(2,1)S(1)} %collective-permute-done.refs_0_.refs_4_) | copy-start | bytes 2359300
  44.1 2.8 %copy-start.1 = (bf16[384,4096]{1,0:T(8,128)(2,1)S(1)}, bf16[384,4096]{1,0:T(8,128)(2,1)}, u32[]{:S(2)}) copy-start(bf16[384,4096]{1,0:T(8,128)(2,1)} %picked_columns.5.refs_0_.refs_1_.refs_2_.refs_3_) | copy-start | bytes 9437188
  46.9 1.8 %collective-permute-start.4 = (f32[384,256]{1,0:T(8,128)S(1)}, f32[384,256]{1,0:T(8,128)S(1)}, u32[]{:S(2)}, u32[]{:S(2)}) collective-permute-start(f32[384,256]{1,0:T(8,128)S(1)} %projected.1), channel_id=1, source_target_pairs={{0,1},{1,0},{2,3},{3,2},{4,5},{5,4},{6,7},{7,6},{8,9},{9,8},{10,11... | collective-permute-start | bytes 1179656 | tf_op jit(solution)/shard_map/ppermute | solution.py:268
  48.7 13.8 %copy-start.4 = (bf16[384,256]{1,0:T(8,128)(2,1)}, bf16[384,256]{1,0:T(8,128)(2,1)S(1)}, u32[]{:S(2)}) copy-start(bf16[384,256]{1,0:T(8,128)(2,1)S(1)} %add_convert_fusion.refs_0_) | copy-start | bytes 589828
  48.7 9.0 %collective-permute-start.6 = (bf16[384,256]{1,0:T(8,128)(2,1)S(1)}, bf16[384,256]{1,0:T(8,128)(2,1)S(1)}, u32[]{:S(2)}, u32[]{:S(2)}) collective-permute-start(bf16[384,256]{1,0:T(8,128)(2,1)S(1)} %add_convert_fusion.refs_0_), channel_id=1, source_target_pairs={{0,4},{1,5},{2,6},{3,7},{4,8},{5,9},{6,10},{7,11},{8,12},{9,13},{1... | collective-permute-start | bytes 589832 | tf_op jit(solution)/shard_map/ppermute | solution.py:274
  52.4 8.7 %collective-permute-start.5 = (bf16[384,256]{1,0:T(8,128)(2,1)S(1)}, bf16[384,256]{1,0:T(8,128)(2,1)S(1)}, u32[]{:S(2)}, u32[]{:S(2)}) collective-permute-start(bf16[384,256]{1,0:T(8,128)(2,1)S(1)} %add_convert_fusion.refs_0_), channel_id=1, source_target_pairs={{0,2},{1,3},{2,4},{3,5},{4,6},{5,7},{6,8},{7,9},{8,10},{9,11},{10,... | collective-permute-start | bytes 589832 | tf_op jit(solution)/shard_map/ppermute | solution.py:274
  54.3 6.8 %collective-permute-start.7 = (bf16[384,256]{1,0:T(8,128)(2,1)S(1)}, bf16[384,256]{1,0:T(8,128)(2,1)S(1)}, u32[]{:S(2)}, u32[]{:S(2)}) collective-permute-start(bf16[384,256]{1,0:T(8,128)(2,1)S(1)} %add_convert_fusion.refs_0_), channel_id=1, source_target_pairs={{0,1},{1,0},{2,3},{3,2},{4,5},{5,4},{6,7},{7,6},{8,9},{9,8},{10,11... | collective-permute-start | bytes 589832 | tf_op jit(solution)/shard_map/ppermute | solution.py:268
  57.7 4.9 %copy-start.6 = (bf16[384,256]{1,0:T(8,128)(2,1)}, bf16[384,256]{1,0:T(8,128)(2,1)S(1)}, u32[]{:S(2)}) copy-start(bf16[384,256]{1,0:T(8,128)(2,1)S(1)} %collective-permute-done.6.refs_2_) | copy-start | bytes 589828
  57.7 3.4 %collective-permute-start.9 = (bf16[384,256]{1,0:T(8,128)(2,1)S(1)}, bf16[384,256]{1,0:T(8,128)(2,1)S(1)}, u32[]{:S(2)}, u32[]{:S(2)}) collective-permute-start(bf16[384,256]{1,0:T(8,128)(2,1)S(1)} %collective-permute-done.6.refs_2_), channel_id=1, source_target_pairs={{0,1},{1,0},{2,3},{3,2},{4,5},{5,4},{6,7},{7,6},{8,9},{9,8},{10,11... | collective-permute-start | bytes 589832 | tf_op jit(solution)/shard_map/ppermute | solution.py:268
  61.1 1.5 copy-start.7
  61.1 1.4 collective-permute-start.8
  61.1 1.4 copy-start.8
  61.1 1.4 copy-start.9
  62.6 0.7 copy-start.10
  86.5 2.0 %collective-permute-start.10 = (bf16[2,384,256]{2,1,0:T(8,128)(2,1)}, bf16[2,384,256]{2,1,0:T(8,128)(2,1)S(1)}, u32[]{:S(2)}, u32[]{:S(2)}) collective-permute-start(bf16[2,384,256]{2,1,0:T(8,128)(2,1)} %get-tuple-element.16), channel_id=1, source_target_pairs={{0,1},{1,0},{2,3},{3,2},{4,5},{5,4},{6,7},{7,6},{8,9},{9,8},{10,11... | collective-permute-start | bytes 1179656 | tf_op jit(solution)/shard_map/ppermute | solution.py:268
  89.6 9.6 %collective-permute-start.11 = (bf16[384,256]{1,0:T(8,128)(2,1)S(1)}, bf16[384,256]{1,0:T(8,128)(2,1)S(1)}, u32[]{:S(2)}, u32[]{:S(2)}) collective-permute-start(bf16[384,256]{1,0:T(8,128)(2,1)S(1)} %get-tuple-element.17), channel_id=1, source_target_pairs={{2,0},{3,1},{4,2},{5,3},{6,4},{7,5},{8,6},{9,7},{10,8},{11,9},{12,... | collective-permute-start | bytes 589832 | tf_op jit(solution)/shard_map/ppermute | solution.py:274
  90.9 12.0 %collective-permute-start.12 = (bf16[384,256]{1,0:T(8,128)(2,1)S(1)}, bf16[384,256]{1,0:T(8,128)(2,1)S(1)}, u32[]{:S(2)}, u32[]{:S(2)}) collective-permute-start(bf16[384,256]{1,0:T(8,128)(2,1)S(1)} %get-tuple-element.18), channel_id=1, source_target_pairs={{4,0},{5,1},{6,2},{7,3},{8,4},{9,5},{10,6},{11,7},{12,8},{13,9},{1... | collective-permute-start | bytes 589832 | tf_op jit(solution)/shard_map/ppermute | solution.py:274
  104.0 1.8 %copy-start.2 = (bf16[384,256]{1,0:T(8,128)(2,1)}, bf16[384,256]{1,0:T(8,128)(2,1)S(1)}, u32[]{:S(2)}) copy-start(bf16[384,256]{1,0:T(8,128)(2,1)S(1)} %fusion.4.refs_8_) | copy-start | bytes 589828
  104.0 1.7 %collective-permute-start.13 = (bf16[384,256]{1,0:T(8,128)(2,1)S(1)}, bf16[384,256]{1,0:T(8,128)(2,1)S(1)}, u32[]{:S(2)}, u32[]{:S(2)}) collective-permute-start(bf16[384,256]{1,0:T(8,128)(2,1)S(1)} %fusion.4.refs_8_), channel_id=1, source_target_pairs={{0,1},{1,0},{2,3},{3,2},{4,5},{5,4},{6,7},{7,6},{8,9},{9,8},{10,11... | collective-permute-start | bytes 589832 | tf_op jit(solution)/shard_map/ppermute | solution.py:268
  105.7 0.7 copy-start.3

commit v2 on v1

--- a/solution.py
+++ b/solution.py
@@ -34,8 +34,14 @@
 
 
 def share_kernel(*refs):
-    chunks = (len(refs) - 3) // 2
-    mine_ref, other_ref, share_ref = refs[-3:]
+    chunks = (len(refs) - 9) // 2
+    terms, (share_ref, mine_ref, other_ref) = refs[2 * chunks : 2 * chunks + 6], refs[2 * chunks + 6 :]
+
+    @pl.when(pl.program_id(0) == 0)
+    def _():
+        for into, (own, near, far) in ((mine_ref, terms[:3]), (other_ref, terms[3:])):
+            into[...] = (own[...] + near[...].astype(F32) + far[...].astype(F32)).astype(BF)
+
     for n in range(chunks):
         both = across(refs[n][...], mine_ref[...]) + across(refs[chunks + n][...], other_ref[...])
         share_ref[n] = both.astype(BF)
@@ -76,24 +82,25 @@
     )(pick, hidden)
 
 
-def chip_share(keep, came, mine, other):
+def chip_share(keep, came, terms):
     rows, width = keep.shape
-    pair = mine.shape[1]
-    chunks = len(came)
-    block = width // (2 * chunks)
+    pair = terms[0].shape[1]
+    chunks, steps = len(came), 2
+    block = width // (steps * chunks)
     whole = pl.BlockSpec((rows, pair), lambda i: (0, 0))
     return pl.pallas_call(
         share_kernel,
-        grid=(2,),
-        in_specs=[pl.BlockSpec((rows, block), lambda i, n=n: (0, 2 * n + i)) for n in range(chunks)]
+        grid=(steps,),
+        in_specs=[pl.BlockSpec((rows, block), lambda i, n=n: (0, steps * n + i)) for n in range(chunks)]
         + [pl.BlockSpec((rows, block), lambda i: (0, i))] * chunks
-        + [whole, whole],
+        + [whole] * len(terms),
         out_specs=pl.BlockSpec((chunks, block, pair), lambda i: (0, i, 0)),
-        out_shape=jax.ShapeDtypeStruct((chunks, 2 * block, pair), BF),
+        out_shape=jax.ShapeDtypeStruct((chunks, steps * block, pair), BF),
+        scratch_shapes=[pltpu.VMEM((rows, pair), BF), pltpu.VMEM((rows, pair), BF)],
         cost_estimate=pl.CostEstimate(flops=4 * width * rows * pair, bytes_accessed=6 * width * rows, transcendentals=0),
-        compiler_params=params(),
+        compiler_params=params(52),
         name="chip_share",
-    )(*([keep] * chunks), *came, mine, other)
+    )(*([keep] * chunks), *came, *terms)
 
 
 def projected(came, weight):
@@ -215,7 +222,7 @@
             into[:, size:] = acc_ref[size:, cols].T.astype(BF)
 
 
-HEADS_PER_STEP = 4
+HEADS_PER_STEP = 8
 
 
 def attention(place, ends, queries, out_grad, pieces):
@@ -287,9 +294,8 @@
     near = (rest[1].astype(F32) + jnp.where(core == 0, third, first)).astype(BF)
     far = (rest[0].astype(F32) + jnp.where(core == 0, 0.0, third)).astype(BF)
     own = rest[2].astype(F32) + jnp.where(core == 0, first, 0.0)
-    summed = own + between_chips(near, -1).astype(F32) + between_chips(far, -2).astype(F32)
-    mine = summed.astype(BF)
-    return mine, between_cores(mine)
+    terms = [own, between_chips(near, -1), between_chips(far, -2)]
+    return terms + [between_cores(term) for term in terms]
 
 
 def per_device(hidden, kv_weight, queries, out_grad, lengths):
@@ -314,8 +320,7 @@
     pieces = window_pieces(key_value)
 
     attended, query_grad, swap, rest = attention(place, ends, queries, out_grad, pieces)
-    mine, other = returned(swap, rest, core)
-    share = chip_share(keep, came, mine, other).reshape(chips, part, pair)
+    share = chip_share(keep, came, returned(swap, rest, core)).reshape(chips, part, pair)
     spread = lax.all_to_all(share, CHIPS, 0, 0, tiled=True)
     return attended, query_grad, jnp.sum(spread.astype(F32), axis=0)
 

time: 156 us -> 152 us (0.974)
  blocking collectives: 42.3 us -> 40.1 us
  Pallas kernels: 50.8 us -> 49.1 us
  waiting for transfers between devices: 29.3 us -> 30.9 us
    all_to_all x1, blocking collectives: 42.3 us -> 40.1 us  [per_device(): spread = lax.all_to_all(share, CHIPS, 0, 0, tiled=True)]
    ppermute x4, waiting for transfers between devices: 17.4 us -> 18.9 us  [between_chips(): return lax.ppermute(block, ALL, route)]
    ppermute x10 -> x12, waiting for transfers between devices: 5.34 us -> 5.33 us  [between_cores(): return lax.ppermute(block, 'core', SWAP)]
  transfers between devices with their start and end apart: 15 -> 17, of which waited for: 9 -> 9; matrix products, arithmetic and copies ran while one was open for 3% -> 3% of each run, Pallas kernels for 12% -> 12%
where the time goes in v2:
time: 152 us
  Pallas kernels  49.1 us (32%)
  blocking collectives  40.1 us (26%)
  waiting for transfers between devices  30.9 us (20%)
  starting transfers between devices  21.2 us (14%)
  other arithmetic  4.58 us (3%)
  local copies, waits for them, and re-layouts  3.86 us (3%)
    all_to_all x1, blocking collectives, per_device(): spread = lax.all_to_all(share, CHIPS, 0, 0, tiled=True)  40.1 us
    pallas_call x1, Pallas kernels, attention(): pl.pallas_call(attention_kernel, grid=(heads // HEADS_PER_STEP,), in_spec...  22 us
    ppermute x4, waiting for transfers between devices, between_chips(): return lax.ppermute(block, ALL, route)  18.9 us
    pallas_call x5, Pallas kernels, picked_columns(): pl.pallas_call(pick_kernel, grid=(steps,), in_specs=[pl.BlockSpec((256, 1...  18.8 us
    all_to_all x1, starting transfers between devices, per_device(): lax.all_to_all(copies, CHIPS, 0, 0, tiled=True).reshape(chips * part, pair)  11.5 us
    ppermute x4, starting transfers between devices, between_chips(): return lax.ppermute(block, ALL, route)  8.17 us
    all_to_all x1, waiting for transfers between devices, per_device(): lax.all_to_all(copies, CHIPS, 0, 0, tiled=True).reshape(chips * part, pair)  6.62 us
    pallas_call x1, Pallas kernels, chip_share(): pl.pallas_call(share_kernel, grid=(steps,), in_specs=[pl.BlockSpec((rows,...  5.63 us
  transfers between devices with their start and end apart: 17, of which 9 were waited for; matrix products, arithmetic and copies ran while one was open for 3% of the time, Pallas kernels for 12%

profile of v2, /device:TPU:0, one launch (start us, length us, event | category | flops | bytes accessed | tf_op | source)
XLA Modules:
  0.0 151.7 jit_solution(5165012660707303388)
XLA Ops:
  0.6 2.4 %broadcast_in_dim.9 = bf16[64,64,256]{2,1,0:T(8,128)(2,1)} broadcast(bf16[64,256]{1,0:T(8,128)(2,1)} %param.6), dimensions={1,2} | broadcast | bytes 2129920 | tf_op jit(solution)/shard_map/broadcast_in_dim | solution.py:307
  3.0 11.5 %all-to-all-start = ((bf16[64,64,256]{2,1,0:T(8,128)(2,1)}), bf16[64,64,256]{2,1,0:T(8,128)(2,1)S(1)}, u32[]{:S(2)}, u32[]{:S(2)}) async-start(bf16[64,64,256]{2,1,0:T(8,128)(2,1)} %broadcast_in_dim.9), calls=%async_computation | async-start | bytes 4194304 | tf_op jit(solution)/shard_map/all_to_all | solution.py:308
  14.5 0.7 fusion.9.pick_ref
  15.2 2.6 %picked_columns.6 = bf16[384,1024]{1,0:T(8,128)(2,1)} custom-call(bf16[256,128]{1,0:T(8,128)(2,1)} %fusion.9.pick_ref, bf16[384,8192]{1,0:T(8,128)(2,1)} %x_ref.9), custom_call_target="tpu_custom_call" | custom-call | bytes 2359296 | tf_op jit(solution)/shard_map/picked_columns/pallas_call | solution.py:70
  17.8 0.0 collective-permute-start
  17.8 2.7 %picked_columns.7 = bf16[384,1024]{1,0:T(8,128)(2,1)} custom-call(bf16[256,128]{1,0:T(8,128)(2,1)} %fusion.9.pick_ref, bf16[384,8192]{1,0:T(8,128)(2,1)} %x_ref.9), custom_call_target="tpu_custom_call" | custom-call | bytes 2359296 | tf_op jit(solution)/shard_map/picked_columns/pallas_call | solution.py:70
  20.5 0.5 collective-permute-start.1
  21.0 2.7 %picked_columns.8 = bf16[384,1024]{1,0:T(8,128)(2,1)} custom-call(bf16[256,128]{1,0:T(8,128)(2,1)} %fusion.9.pick_ref, bf16[384,8192]{1,0:T(8,128)(2,1)} %x_ref.9), custom_call_target="tpu_custom_call" | custom-call | bytes 2359296 | tf_op jit(solution)/shard_map/picked_columns/pallas_call | solution.py:70
  23.7 0.0 collective-permute-start.2
  23.7 2.7 %picked_columns.9 = bf16[384,1024]{1,0:T(8,128)(2,1)} custom-call(bf16[256,128]{1,0:T(8,128)(2,1)} %fusion.9.pick_ref, bf16[384,8192]{1,0:T(8,128)(2,1)} %x_ref.9), custom_call_target="tpu_custom_call" | custom-call | bytes 2359296 | tf_op jit(solution)/shard_map/picked_columns/pallas_call | solution.py:70
  26.4 0.5 collective-permute-start.3
  26.8 0.0 copy-done.3
  26.9 0.3 reduce-window.9
  27.2 0.1 slice.25
  27.3 0.1 slice_reduce_fusion
  27.4 0.1 add_bitcast_fusion
  27.5 0.6 broadcast_in_dim.8.ends_ref
  28.1 0.7 fusion.8.pick_ref
  28.7 8.1 %picked_columns.5.refs_0_.refs_1_.refs_2_.refs_3_ = bf16[384,4096]{1,0:T(8,128)(2,1)} custom-call(bf16[256,128]{1,0:T(8,128)(2,1)} %fusion.8.pick_ref, bf16[384,8192]{1,0:T(8,128)(2,1)} %x_ref.9), custom_call_target="tpu_custom_call" | custom-call | bytes 9437184 | tf_op jit(solution)/shard_map/picked_columns/pallas_call | solution.py:70
  36.9 0.6 pad_add_fusion.place_ref
  37.5 0.0 collective-permute-done.refs_0_.refs_4_
  37.5 0.0 collective-permute-done.1.refs_1_.refs_5_
  37.5 0.0 collective-permute-done.2.refs_2_.refs_6_
  37.5 0.0 collective-permute-done.3.refs_3_.refs_7_
  37.5 6.6 %all-to-all-done = bf16[64,64,256]{2,1,0:T(8,128)(2,1)S(1)} async-done(((bf16[64,64,256]{2,1,0:T(8,128)(2,1)}), bf16[64,64,256]{2,1,0:T(8,128)(2,1)S(1)}, u32[]{:S(2)}, u32[]{:S(2)}) %all-to-all-start) | async-done | bytes 2097184 | tf_op jit(solution)/shard_map/all_to_all | solution.py:308
  44.1 2.7 %projected.1 = f32[384,256]{1,0:T(8,128)S(1)} custom-call(bf16[384,1024]{1,0:T(8,128)(2,1)S(1)} %collective-permute-done.refs_0_.refs_4_, bf16[384,1024]{1,0:T(8,128)(2,1)} %collective-permute-done.1.refs_1_.refs_5_, bf16[384,1024]{1,0:T(8,128)(2,1)} %collective-permute-done.2.refs_2_.refs_6_, bf16[384,1024]{1,0:T(8,128)(2,1)} %collective-permute-done.3.refs_3_.refs_7_, ...), custom_call_target="tpu_custom_call" | custom-call | flops 805306368 | bytes 2097152 | tf_op jit(solution)/shard_map/projected/pallas_call | solution.py:108
  46.8 0.0 copy-done
  46.9 0.1 collective-permute-start.4
  46.9 0.0 copy-done.1
  47.0 1.0 fusion.11
  48.0 0.7 collective-permute-done.4
  48.7 0.1 add_convert_fusion.refs_0_
  48.7 0.0 copy-start.2
  48.7 3.7 %collective-permute-start.6 = (bf16[384,256]{1,0:T(8,128)(2,1)S(1)}, bf16[384,256]{1,0:T(8,128)(2,1)S(1)}, u32[]{:S(2)}, u32[]{:S(2)}) collective-permute-start(bf16[384,256]{1,0:T(8,128)(2,1)S(1)} %add_convert_fusion.refs_0_), channel_id=1, source_target_pairs={{0,4},{1,5},{2,6},{3,7},{4,8},{5,9},{6,10},{7,11},{8,12},{9,13},{1... | collective-permute-start | bytes 589832 | tf_op jit(solution)/shard_map/ppermute | solution.py:281
  52.4 1.9 %collective-permute-start.5 = (bf16[384,256]{1,0:T(8,128)(2,1)S(1)}, bf16[384,256]{1,0:T(8,128)(2,1)S(1)}, u32[]{:S(2)}, u32[]{:S(2)}) collective-permute-start(bf16[384,256]{1,0:T(8,128)(2,1)S(1)} %add_convert_fusion.refs_0_), channel_id=1, source_target_pairs={{0,2},{1,3},{2,4},{3,5},{4,6},{5,7},{6,8},{7,9},{8,10},{9,11},{10,... | collective-permute-start | bytes 589832 | tf_op jit(solution)/shard_map/ppermute | solution.py:281
  54.3 0.1 collective-permute-start.7
  54.4 3.3 %collective-permute-done.6.refs_2_ = bf16[384,256]{1,0:T(8,128)(2,1)S(1)} collective-permute-done((bf16[384,256]{1,0:T(8,128)(2,1)S(1)}, bf16[384,256]{1,0:T(8,128)(2,1)S(1)}, u32[]{:S(2)}, u32[]{:S(2)}) %collective-permute-start.6) | collective-permute-done | bytes 196640 | tf_op jit(solution)/shard_map/ppermute | solution.py:281
  57.7 0.0 collective-permute-start.9
  57.7 3.4 %collective-permute-done.5.refs_1_ = bf16[384,256]{1,0:T(8,128)(2,1)S(1)} collective-permute-done((bf16[384,256]{1,0:T(8,128)(2,1)S(1)}, bf16[384,256]{1,0:T(8,128)(2,1)S(1)}, u32[]{:S(2)}, u32[]{:S(2)}) %collective-permute-start.5) | collective-permute-done | bytes 196640 | tf_op jit(solution)/shard_map/ppermute | solution.py:281
  61.1 0.0 collective-permute-start.8
  61.1 0.0 collective-permute-done.7.refs_3_
  61.1 0.0 copy-start.6
  61.1 0.0 collective-permute-done.9.refs_5_
  61.1 0.0 copy-start.7
  61.1 1.4 collective-permute-done.8.refs_4_
  62.5 0.0 copy-done.4
  62.6 0.7 copy-done.8
  63.2 22.0 %attention.1 = (bf16[384,1024]{1,0:T(8,128)(2,1)}, bf16[384,1024]{1,0:T(8,128)(2,1)}, bf16[2,384,256]{2,1,0:T(8,128)(2,1)}, bf16[3,384,256]{2,1,0:T(8,128)(2,1)}) custom-call(s32[2]{0:T(128)} %pad_add_fusion.place_ref, s32[1,264]{1,0:T(1,128)} %broadcast_in_dim.8.ends_ref, bf16[384,1024]{1,0:T(8,128)(2,1)} %q_ref.1, bf16[384,1024]{1,0:T(8,128)(2,1)} %g_ref.1, ...), custom_call_target="tpu_custom_call" | custom-call | flops 18119393280 | bytes 3932160 | tf_op jit(solution)/shard_map/attention/pallas_call | solution.py:236
  85.2 0.1 collective-permute-start.10
  85.3 1.8 %collective-permute-done.10 = bf16[2,384,256]{2,1,0:T(8,128)(2,1)S(1)} collective-permute-done((bf16[2,384,256]{2,1,0:T(8,128)(2,1)}, bf16[2,384,256]{2,1,0:T(8,128)(2,1)S(1)}, u32[]{:S(2)}, u32[]{:S(2)}) %collective-permute-start.10) | collective-permute-done | bytes 393248 | tf_op jit(solution)/shard_map/ppermute | solution.py:275
  87.1 1.3 fusion.6
  88.4 1.3 collective-permute-start.12
  89.7 1.3 collective-permute-start.11
  91.0 0.2 collective-permute-start.13
  91.2 8.3 %collective-permute-done.12.refs_10_ = bf16[384,256]{1,0:T(8,128)(2,1)S(1)} collective-permute-done((bf16[384,256]{1,0:T(8,128)(2,1)S(1)}, bf16[384,256]{1,0:T(8,128)(2,1)S(1)}, u32[]{:S(2)}, u32[]{:S(2)}) %collective-permute-start.12) | collective-permute-done | bytes 196640 | tf_op jit(solution)/shard_map/ppermute | solution.py:281
  99.5 0.0 collective-permute-start.15
  99.5 4.0 %collective-permute-done.11.refs_9_ = bf16[384,256]{1,0:T(8,128)(2,1)S(1)} collective-permute-done((bf16[384,256]{1,0:T(8,128)(2,1)S(1)}, bf16[384,256]{1,0:T(8,128)(2,1)S(1)}, u32[]{:S(2)}, u32[]{:S(2)}) %collective-permute-start.11) | collective-permute-done | bytes 196640 | tf_op jit(solution)/shard_map/ppermute | solution.py:281
  103.5 0.0 collective-permute-start.14
  103.5 0.0 collective-permute-done.15.refs_13_
  103.5 1.4 collective-permute-done.14.refs_12_
  105.0 0.0 collective-permute-done.13.refs_11_
  105.0 5.6 %chip_share.1 = bf16[4,1024,256]{2,1,0:T(8,128)(2,1)} custom-call(bf16[384,4096]{1,0:T(8,128)(2,1)} %picked_columns.5.refs_0_.refs_1_.refs_2_.refs_3_, bf16[384,4096]{1,0:T(8,128)(2,1)} %picked_columns.5.refs_0_.refs_1_.refs_2_.refs_3_, bf16[384,4096]{1,0:T(8,128)(2,1)} %picked_columns.5.refs_0_.refs_1_.refs_2_.refs_3_, ...), custom_call_target="tpu_custom_call" | custom-call | flops 1610612736 | bytes 9437184 | tf_op jit(solution)/shard_map/chip_share/pallas_call | solution.py:91
  110.6 40.1 %all_to_all.10 = bf16[64,64,256]{2,1,0:T(8,128)(2,1)S(1)} all-to-all(bf16[64,64,256]{2,1,0:T(8,128)(2,1)} %bitcast.19), channel_id=1, replica_groups=mesh['z'=4,'x'=4,'y'=4,'core'=2] {'z','x','y'}, dimensions={0} | all-to-all | bytes 4194304 | tf_op jit(solution)/shard_map/all_to_all | solution.py:324
  150.7 0.9 convert_reduce_fusion
  (14 shorter events, 0.1 us)
Async XLA Ops:
  3.0 41.1 %all-to-all-start = ((bf16[64,64,256]{2,1,0:T(8,128)(2,1)}), bf16[64,64,256]{2,1,0:T(8,128)(2,1)S(1)}, u32[]{:S(2)}, u32[]{:S(2)}) async-start(bf16[64,64,256]{2,1,0:T(8,128)(2,1)} %broadcast_in_dim.9), calls=%async_computation | async-start | bytes 4194304 | tf_op jit(solution)/shard_map/all_to_all | solution.py:308
  17.8 19.6 %collective-permute-start = (bf16[384,1024]{1,0:T(8,128)(2,1)}, bf16[384,1024]{1,0:T(8,128)(2,1)S(1)}, u32[]{:S(2)}, u32[]{:S(2)}) collective-permute-start(bf16[384,1024]{1,0:T(8,128)(2,1)} %picked_columns.6), channel_id=1, source_target_pairs={{0,1},{1,0},{2,3},{3,2},{4,5},{5,4},{6,7},{7,6},{8,9},{9,8},{10,11... | collective-permute-start | bytes 2359304 | tf_op jit(solution)/shard_map/ppermute | solution.py:275
  20.5 17.0 %collective-permute-start.1 = (bf16[384,1024]{1,0:T(8,128)(2,1)}, bf16[384,1024]{1,0:T(8,128)(2,1)}, u32[]{:S(2)}, u32[]{:S(2)}) collective-permute-start(bf16[384,1024]{1,0:T(8,128)(2,1)} %picked_columns.7), channel_id=1, source_target_pairs={{0,1},{1,0},{2,3},{3,2},{4,5},{5,4},{6,7},{7,6},{8,9},{9,8},{10,11... | collective-permute-start | bytes 2359304 | tf_op jit(solution)/shard_map/ppermute | solution.py:275
  23.7 3.2 %copy-start.3 = (s32[264]{0:T(512)S(1)}, s32[264]{0:T(512)}, u32[]{:S(2)}) copy-start(s32[264]{0:T(512)} %param.9) | copy-start | bytes 3172
  23.7 13.8 %collective-permute-start.2 = (bf16[384,1024]{1,0:T(8,128)(2,1)}, bf16[384,1024]{1,0:T(8,128)(2,1)}, u32[]{:S(2)}, u32[]{:S(2)}) collective-permute-start(bf16[384,1024]{1,0:T(8,128)(2,1)} %picked_columns.8), channel_id=1, source_target_pairs={{0,1},{1,0},{2,3},{3,2},{4,5},{5,4},{6,7},{7,6},{8,9},{9,8},{10,11... | collective-permute-start | bytes 2359304 | tf_op jit(solution)/shard_map/ppermute | solution.py:275
  26.4 11.1 %collective-permute-start.3 = (bf16[384,1024]{1,0:T(8,128)(2,1)}, bf16[384,1024]{1,0:T(8,128)(2,1)}, u32[]{:S(2)}, u32[]{:S(2)}) collective-permute-start(bf16[384,1024]{1,0:T(8,128)(2,1)} %picked_columns.9), channel_id=1, source_target_pairs={{0,1},{1,0},{2,3},{3,2},{4,5},{5,4},{6,7},{7,6},{8,9},{9,8},{10,11... | collective-permute-start | bytes 2359304 | tf_op jit(solution)/shard_map/ppermute | solution.py:275
  37.5 9.4 %copy-start = (bf16[384,1024]{1,0:T(8,128)(2,1)}, bf16[384,1024]{1,0:T(8,128)(2,1)S(1)}, u32[]{:S(2)}) copy-start(bf16[384,1024]{1,0:T(8,128)(2,1)S(1)} %collective-permute-done.refs_0_.refs_4_) | copy-start | bytes 2359300
  44.1 2.8 %copy-start.1 = (bf16[384,4096]{1,0:T(8,128)(2,1)S(1)}, bf16[384,4096]{1,0:T(8,128)(2,1)}, u32[]{:S(2)}) copy-start(bf16[384,4096]{1,0:T(8,128)(2,1)} %picked_columns.5.refs_0_.refs_1_.refs_2_.refs_3_) | copy-start | bytes 9437188
  46.9 1.8 %collective-permute-start.4 = (f32[384,256]{1,0:T(8,128)S(1)}, f32[384,256]{1,0:T(8,128)S(1)}, u32[]{:S(2)}, u32[]{:S(2)}) collective-permute-start(f32[384,256]{1,0:T(8,128)S(1)} %projected.1), channel_id=1, source_target_pairs={{0,1},{1,0},{2,3},{3,2},{4,5},{5,4},{6,7},{7,6},{8,9},{9,8},{10,11... | collective-permute-start | bytes 1179656 | tf_op jit(solution)/shard_map/ppermute | solution.py:275
  48.7 13.8 %copy-start.2 = (bf16[384,256]{1,0:T(8,128)(2,1)}, bf16[384,256]{1,0:T(8,128)(2,1)S(1)}, u32[]{:S(2)}) copy-start(bf16[384,256]{1,0:T(8,128)(2,1)S(1)} %add_convert_fusion.refs_0_) | copy-start | bytes 589828
  48.7 9.0 %collective-permute-start.6 = (bf16[384,256]{1,0:T(8,128)(2,1)S(1)}, bf16[384,256]{1,0:T(8,128)(2,1)S(1)}, u32[]{:S(2)}, u32[]{:S(2)}) collective-permute-start(bf16[384,256]{1,0:T(8,128)(2,1)S(1)} %add_convert_fusion.refs_0_), channel_id=1, source_target_pairs={{0,4},{1,5},{2,6},{3,7},{4,8},{5,9},{6,10},{7,11},{8,12},{9,13},{1... | collective-permute-start | bytes 589832 | tf_op jit(solution)/shard_map/ppermute | solution.py:281
  52.4 8.7 %collective-permute-start.5 = (bf16[384,256]{1,0:T(8,128)(2,1)S(1)}, bf16[384,256]{1,0:T(8,128)(2,1)S(1)}, u32[]{:S(2)}, u32[]{:S(2)}) collective-permute-start(bf16[384,256]{1,0:T(8,128)(2,1)S(1)} %add_convert_fusion.refs_0_), channel_id=1, source_target_pairs={{0,2},{1,3},{2,4},{3,5},{4,6},{5,7},{6,8},{7,9},{8,10},{9,11},{10,... | collective-permute-start | bytes 589832 | tf_op jit(solution)/shard_map/ppermute | solution.py:281
  54.3 6.8 %collective-permute-start.7 = (bf16[384,256]{1,0:T(8,128)(2,1)S(1)}, bf16[384,256]{1,0:T(8,128)(2,1)S(1)}, u32[]{:S(2)}, u32[]{:S(2)}) collective-permute-start(bf16[384,256]{1,0:T(8,128)(2,1)S(1)} %add_convert_fusion.refs_0_), channel_id=1, source_target_pairs={{0,1},{1,0},{2,3},{3,2},{4,5},{5,4},{6,7},{7,6},{8,9},{9,8},{10,11... | collective-permute-start | bytes 589832 | tf_op jit(solution)/shard_map/ppermute | solution.py:275
  57.7 4.9 %copy-start.4 = (bf16[384,256]{1,0:T(8,128)(2,1)}, bf16[384,256]{1,0:T(8,128)(2,1)S(1)}, u32[]{:S(2)}) copy-start(bf16[384,256]{1,0:T(8,128)(2,1)S(1)} %collective-permute-done.6.refs_2_) | copy-start | bytes 589828
  57.7 3.4 %collective-permute-start.9 = (bf16[384,256]{1,0:T(8,128)(2,1)S(1)}, bf16[384,256]{1,0:T(8,128)(2,1)S(1)}, u32[]{:S(2)}, u32[]{:S(2)}) collective-permute-start(bf16[384,256]{1,0:T(8,128)(2,1)S(1)} %collective-permute-done.6.refs_2_), channel_id=1, source_target_pairs={{0,1},{1,0},{2,3},{3,2},{4,5},{5,4},{6,7},{7,6},{8,9},{9,8},{10,11... | collective-permute-start | bytes 589832 | tf_op jit(solution)/shard_map/ppermute | solution.py:275
  61.1 1.5 copy-start.5
  61.1 1.4 collective-permute-start.8
  61.1 1.4 copy-start.6
  61.1 1.4 copy-start.7
  62.6 0.7 copy-start.8
  85.2 1.9 %collective-permute-start.10 = (bf16[2,384,256]{2,1,0:T(8,128)(2,1)}, bf16[2,384,256]{2,1,0:T(8,128)(2,1)S(1)}, u32[]{:S(2)}, u32[]{:S(2)}) collective-permute-start(bf16[2,384,256]{2,1,0:T(8,128)(2,1)} %get-tuple-element.16), channel_id=1, source_target_pairs={{0,1},{1,0},{2,3},{3,2},{4,5},{5,4},{6,7},{7,6},{8,9},{9,8},{10,11... | collective-permute-start | bytes 1179656 | tf_op jit(solution)/shard_map/ppermute | solution.py:275
  88.4 11.1 %collective-permute-start.12 = (bf16[384,256]{1,0:T(8,128)(2,1)S(1)}, bf16[384,256]{1,0:T(8,128)(2,1)S(1)}, u32[]{:S(2)}, u32[]{:S(2)}) collective-permute-start(bf16[384,256]{1,0:T(8,128)(2,1)S(1)} %get-tuple-element.17), channel_id=1, source_target_pairs={{4,0},{5,1},{6,2},{7,3},{8,4},{9,5},{10,6},{11,7},{12,8},{13,9},{1... | collective-permute-start | bytes 589832 | tf_op jit(solution)/shard_map/ppermute | solution.py:281
  89.7 13.8 %collective-permute-start.11 = (bf16[384,256]{1,0:T(8,128)(2,1)S(1)}, bf16[384,256]{1,0:T(8,128)(2,1)S(1)}, u32[]{:S(2)}, u32[]{:S(2)}) collective-permute-start(bf16[384,256]{1,0:T(8,128)(2,1)S(1)} %get-tuple-element.18), channel_id=1, source_target_pairs={{2,0},{3,1},{4,2},{5,3},{6,4},{7,5},{8,6},{9,7},{10,8},{11,9},{12,... | collective-permute-start | bytes 589832 | tf_op jit(solution)/shard_map/ppermute | solution.py:281
  91.0 14.0 %collective-permute-start.13 = (f32[384,256]{1,0:T(8,128)S(1)}, f32[384,256]{1,0:T(8,128)S(1)}, u32[]{:S(2)}, u32[]{:S(2)}) collective-permute-start(f32[384,256]{1,0:T(8,128)S(1)} %get-tuple-element.19.refs_8_), channel_id=1, source_target_pairs={{0,1},{1,0},{2,3},{3,2},{4,5},{5,4},{6,7},{7,6},{8,9},{9,8},{10,11... | collective-permute-start | bytes 1179656 | tf_op jit(solution)/shard_map/ppermute | solution.py:275
  99.5 4.0 %collective-permute-start.15 = (bf16[384,256]{1,0:T(8,128)(2,1)S(1)}, bf16[384,256]{1,0:T(8,128)(2,1)S(1)}, u32[]{:S(2)}, u32[]{:S(2)}) collective-permute-start(bf16[384,256]{1,0:T(8,128)(2,1)S(1)} %collective-permute-done.12.refs_10_), channel_id=1, source_target_pairs={{0,1},{1,0},{2,3},{3,2},{4,5},{5,4},{6,7},{7,6},{8,9},{9,8},{10,11... | collective-permute-start | bytes 589832 | tf_op jit(solution)/shard_map/ppermute | solution.py:275
  103.5 1.4 collective-permute-start.14

commit v3 on v2

--- a/solution.py
+++ b/solution.py
@@ -135,36 +135,42 @@
     return [block[:, n : n + size] for n in range(0, block.shape[1], size)]
 
 
-def attention_kernel(place_ref, ends_ref, q_ref, g_ref, *refs):
+def attention_kernel(place_ref, ends_ref, q_hbm, g_hbm, *refs):
     pieces = refs[:PIECES]
-    out_ref, dq_ref, swap_ref, rest_ref, kv_ref, turned_ref, bias_ref, s_ref, p_ref, acc_ref = refs[PIECES:]
-    step = pl.program_id(0)
+    out_hbm, dq_hbm, swap_ref, rest_ref, kv_ref, turned_ref, bias_ref, s_ref, p_ref, acc_ref, *refs = refs[PIECES:]
+    q_ref, g_ref, out_ref, dq_ref, sems = refs
     rows = q_ref.shape[0]
     size = kv_ref.shape[1] // 2
     span = kv_ref.shape[0]
+    heads = q_ref.shape[1] // size
+
+    arriving = [pltpu.make_async_copy(q_hbm, q_ref, sems.at[0]), pltpu.make_async_copy(g_hbm, g_ref, sems.at[1])]
+    leaving = [pltpu.make_async_copy(out_ref, out_hbm, sems.at[2]), pltpu.make_async_copy(dq_ref, dq_hbm, sems.at[3])]
+    for copy in arriving:
+        copy.start()
     chunks = key_chunks(rows)
     scale = 1.0 / math.sqrt(size)
     scale2 = scale * math.log2(math.e)
 
-    @pl.when(step == 0)
-    def _():
-        offset, core, ends = place_ref[0], place_ref[1], ends_ref[...]
-        position = offset + lax.broadcasted_iota(jnp.int32, (rows, ends.shape[1]), 0)
-        start = jnp.max(jnp.where(ends <= position, ends, 0), axis=1, keepdims=True)
-        low = start - (offset - SPAN * rows)
-        row = lax.broadcasted_iota(jnp.int32, (rows, rows), 0)
-        own, second, fourth, other_own, other_second, other_fourth = [piece[...] for piece in pieces]
-        first = jnp.where(core == 0, other_second, other_own)
-        third = jnp.where(core == 0, other_fourth, other_second)
-        for j, piece in enumerate([fourth, third, second, first, own]):
-            cols = slice(j * rows, (j + 1) * rows)
-            kv_ref[cols, :] = piece
-            turned_ref[:size, cols] = piece[:, :size].T
-            turned_ref[size:, cols] = piece[:, size:].T
-            at = lax.broadcasted_iota(jnp.int32, (rows, rows), 1) + j * rows
-            allowed = (at >= low) & (at <= row + SPAN * rows)
-            bias_ref[:, cols] = jnp.where(allowed, 0.0, NEG)
-        acc_ref[...] = jnp.zeros_like(acc_ref)
+    offset, core, ends = place_ref[0], place_ref[1], ends_ref[...]
+    position = offset + lax.broadcasted_iota(jnp.int32, (rows, ends.shape[1]), 0)
+    start = jnp.max(jnp.where(ends <= position, ends, 0), axis=1, keepdims=True)
+    low = start - (offset - SPAN * rows)
+    row = lax.broadcasted_iota(jnp.int32, (rows, rows), 0)
+    own, second, fourth, other_own, other_second, other_fourth = [piece[...] for piece in pieces]
+    first = jnp.where(core == 0, other_second, other_own)
+    third = jnp.where(core == 0, other_fourth, other_second)
+    for j, piece in enumerate([fourth, third, second, first, own]):
+        cols = slice(j * rows, (j + 1) * rows)
+        kv_ref[cols, :] = piece
+        turned_ref[:size, cols] = piece[:, :size].T
+        turned_ref[size:, cols] = piece[:, size:].T
+        at = lax.broadcasted_iota(jnp.int32, (rows, rows), 1) + j * rows
+        allowed = (at >= low) & (at <= row + SPAN * rows)
+        bias_ref[:, cols] = jnp.where(allowed, 0.0, NEG)
+    acc_ref[...] = jnp.zeros_like(acc_ref)
+    for copy in arriving:
+        copy.wait()
 
     def one_head(h):
         lanes = slice(h * size, (h + 1) * size)
@@ -206,23 +212,22 @@
             yield
         dq_ref[:, lanes] = (dq * scale).astype(BF)
 
-    running, waiting = [], [one_head(h) for h in range(q_ref.shape[1] // size)]
+    running, waiting = [], [one_head(h) for h in range(heads)]
     while running or waiting:
         if waiting:
             running.append(waiting.pop(0))
         for _ in chunks:
             running = [head for head in running if next(head, head) is None]
 
-    @pl.when(step == pl.num_programs(0) - 1)
-    def _():
-        for j in range(SPAN + 1):
-            cols = slice(j * rows, (j + 1) * rows)
-            into = rest_ref.at[j // 2] if j % 2 == 0 else swap_ref.at[1 - j // 2]
-            into[:, :size] = (acc_ref[:size, cols].T * scale).astype(BF)
-            into[:, size:] = acc_ref[size:, cols].T.astype(BF)
-
-
-HEADS_PER_STEP = 8
+    for copy in leaving:
+        copy.start()
+    for j in range(SPAN + 1):
+        cols = slice(j * rows, (j + 1) * rows)
+        into = rest_ref.at[j // 2] if j % 2 == 0 else swap_ref.at[1 - j // 2]
+        into[:, :size] = (acc_ref[:size, cols].T * scale).astype(BF)
+        into[:, size:] = acc_ref[size:, cols].T.astype(BF)
+    for copy in leaving:
+        copy.wait()
 
 
 def attention(place, ends, queries, out_grad, pieces):
@@ -231,24 +236,12 @@
     size = pair // 2
     heads = width // size
     span = (SPAN + 1) * rows
-    several = pl.BlockSpec((rows, HEADS_PER_STEP * size), lambda h: (0, h))
-    whole = pl.BlockSpec((rows, pair), lambda h: (0, 0))
+    far_off = pl.BlockSpec(memory_space=pltpu.HBM)
+    near_by = pl.BlockSpec(memory_space=pltpu.VMEM)
     return pl.pallas_call(
         attention_kernel,
-        grid=(heads // HEADS_PER_STEP,),
-        in_specs=[
-            pl.BlockSpec(memory_space=pltpu.SMEM),
-            pl.BlockSpec((1, ends.shape[1]), lambda h: (0, 0)),
-            several,
-            several,
-        ]
-        + [whole] * PIECES,
-        out_specs=[
-            several,
-            several,
-            pl.BlockSpec((SPAN // 2, rows, pair), lambda h: (0, 0, 0)),
-            pl.BlockSpec((SPAN // 2 + 1, rows, pair), lambda h: (0, 0, 0)),
-        ],
+        in_specs=[pl.BlockSpec(memory_space=pltpu.SMEM), near_by, far_off, far_off] + [near_by] * PIECES,
+        out_specs=[far_off, far_off, near_by, near_by],
         out_shape=[
             jax.ShapeDtypeStruct((rows, width), BF),
             jax.ShapeDtypeStruct((rows, width), BF),
@@ -262,11 +255,16 @@
             pltpu.VMEM((2, rows, span), F32),
             pltpu.VMEM((2, rows, span), BF),
             pltpu.VMEM((pair, span), F32),
+            pltpu.VMEM((rows, width), BF),
+            pltpu.VMEM((rows, width), BF),
+            pltpu.VMEM((rows, width), BF),
+            pltpu.VMEM((rows, width), BF),
+            pltpu.SemaphoreType.DMA((4,)),
         ],
         cost_estimate=pl.CostEstimate(
             flops=24 * heads * rows * span * size, bytes_accessed=10 * rows * width, transcendentals=heads * rows * span
         ),
-        compiler_params=params(56),
+        compiler_params=params(36),
         name="attention",
     )(place, ends, queries, out_grad, *pieces)
 

time: 152 us -> 150 us (0.987)
  other arithmetic: 4.58 us -> 2.96 us
  transfers between devices with their start and end apart: 17 -> 17, of which waited for: 9 -> 9; matrix products, arithmetic and copies ran while one was open for 3% -> 2% of each run, Pallas kernels for 12% -> 13%
where the time goes in v3:
time: 150 us; the launch traced here: 149 us
  Pallas kernels  48.6 us (32%)
  blocking collectives  40.1 us (27%)
  waiting for transfers between devices  31.8 us (21%)
  starting transfers between devices  21.3 us (14%)
  other arithmetic  2.96 us (2%)
  local copies, waits for them, and re-layouts  2.6 us (2%)
    all_to_all x1, blocking collectives, per_device(): spread = lax.all_to_all(share, CHIPS, 0, 0, tiled=True)  40.1 us
    pallas_call x1, Pallas kernels, attention(): pl.pallas_call(attention_kernel, in_specs=[pl.BlockSpec(memory_space=pltp...  21.4 us
    ppermute x4, waiting for transfers between devices, between_chips(): return lax.ppermute(block, ALL, route)  18.9 us
    pallas_call x5, Pallas kernels, picked_columns(): pl.pallas_call(pick_kernel, grid=(steps,), in_specs=[pl.BlockSpec((256, 1...  18.9 us
    all_to_all x1, starting transfers between devices, per_device(): lax.all_to_all(copies, CHIPS, 0, 0, tiled=True).reshape(chips * part, pair)  11.5 us
    ppermute x4, starting transfers between devices, between_chips(): return lax.ppermute(block, ALL, route)  8.17 us
    all_to_all x1, waiting for transfers between devices, per_device(): lax.all_to_all(copies, CHIPS, 0, 0, tiled=True).reshape(chips * part, pair)  7.66 us
    pallas_call x1, Pallas kernels, chip_share(): pl.pallas_call(share_kernel, grid=(steps,), in_specs=[pl.BlockSpec((rows,...  5.62 us
  transfers between devices with their start and end apart: 17, of which 9 were waited for; matrix products, arithmetic and copies ran while one was open for 2% of the time, Pallas kernels for 13%

profile of v3, /device:TPU:0, one launch (start us, length us, event | category | flops | bytes accessed | tf_op | source)
XLA Modules:
  0.0 149.2 jit_solution(14276438853225181045)
XLA Ops:
  0.6 2.4 %broadcast_in_dim.9 = bf16[64,64,256]{2,1,0:T(8,128)(2,1)} broadcast(bf16[64,256]{1,0:T(8,128)(2,1)} %param.6), dimensions={1,2} | broadcast | bytes 2129920 | tf_op jit(solution)/shard_map/broadcast_in_dim | solution.py:305
  3.0 11.5 %all-to-all-start = ((bf16[64,64,256]{2,1,0:T(8,128)(2,1)}), bf16[64,64,256]{2,1,0:T(8,128)(2,1)S(1)}, u32[]{:S(2)}, u32[]{:S(2)}) async-start(bf16[64,64,256]{2,1,0:T(8,128)(2,1)} %broadcast_in_dim.9), calls=%async_computation | async-start | bytes 4194304 | tf_op jit(solution)/shard_map/all_to_all | solution.py:306
  14.5 0.7 fusion.9.pick_ref
  15.2 2.6 %picked_columns.6 = bf16[384,1024]{1,0:T(8,128)(2,1)} custom-call(bf16[256,128]{1,0:T(8,128)(2,1)} %fusion.9.pick_ref, bf16[384,8192]{1,0:T(8,128)(2,1)} %x_ref.9), custom_call_target="tpu_custom_call" | custom-call | bytes 2359296 | tf_op jit(solution)/shard_map/picked_columns/pallas_call | solution.py:70
  17.8 0.0 collective-permute-start
  17.8 2.7 %picked_columns.7 = bf16[384,1024]{1,0:T(8,128)(2,1)} custom-call(bf16[256,128]{1,0:T(8,128)(2,1)} %fusion.9.pick_ref, bf16[384,8192]{1,0:T(8,128)(2,1)} %x_ref.9), custom_call_target="tpu_custom_call" | custom-call | bytes 2359296 | tf_op jit(solution)/shard_map/picked_columns/pallas_call | solution.py:70
  20.5 0.5 collective-permute-start.1
  21.0 2.7 %picked_columns.8 = bf16[384,1024]{1,0:T(8,128)(2,1)} custom-call(bf16[256,128]{1,0:T(8,128)(2,1)} %fusion.9.pick_ref, bf16[384,8192]{1,0:T(8,128)(2,1)} %x_ref.9), custom_call_target="tpu_custom_call" | custom-call | bytes 2359296 | tf_op jit(solution)/shard_map/picked_columns/pallas_call | solution.py:70
  23.7 0.0 copy-start.4
  23.7 0.0 collective-permute-start.2
  23.7 2.7 %picked_columns.9 = bf16[384,1024]{1,0:T(8,128)(2,1)} custom-call(bf16[256,128]{1,0:T(8,128)(2,1)} %fusion.9.pick_ref, bf16[384,8192]{1,0:T(8,128)(2,1)} %x_ref.9), custom_call_target="tpu_custom_call" | custom-call | bytes 2359296 | tf_op jit(solution)/shard_map/picked_columns/pallas_call | solution.py:70
  26.4 0.5 collective-permute-start.3
  26.9 0.0 copy-done.4
  26.9 0.3 reduce-window.9
  27.2 0.1 slice.25
  27.3 0.1 slice_reduce_fusion
  27.4 0.1 add_bitcast_fusion
  27.5 0.7 fusion.8.pick_ref
  28.2 8.2 %picked_columns.5.refs_0_.refs_1_.refs_2_.refs_3_ = bf16[384,4096]{1,0:T(8,128)(2,1)} custom-call(bf16[256,128]{1,0:T(8,128)(2,1)} %fusion.8.pick_ref, bf16[384,8192]{1,0:T(8,128)(2,1)} %x_ref.9), custom_call_target="tpu_custom_call" | custom-call | bytes 9437184 | tf_op jit(solution)/shard_map/picked_columns/pallas_call | solution.py:70
  36.3 0.1 pad_add_fusion.place_ref
  36.4 0.0 collective-permute-done.refs_0_.refs_4_
  36.4 0.0 copy-start
  36.4 0.0 collective-permute-done.1.refs_1_.refs_5_
  36.4 0.0 collective-permute-done.2.refs_2_.refs_6_
  36.4 0.0 collective-permute-done.3.refs_3_.refs_7_
  36.5 7.7 %all-to-all-done = bf16[64,64,256]{2,1,0:T(8,128)(2,1)S(1)} async-done(((bf16[64,64,256]{2,1,0:T(8,128)(2,1)}), bf16[64,64,256]{2,1,0:T(8,128)(2,1)S(1)}, u32[]{:S(2)}, u32[]{:S(2)}) %all-to-all-start) | async-done | bytes 2097184 | tf_op jit(solution)/shard_map/all_to_all | solution.py:306
  44.1 2.7 %projected.1 = f32[384,256]{1,0:T(8,128)S(1)} custom-call(bf16[384,1024]{1,0:T(8,128)(2,1)S(1)} %collective-permute-done.refs_0_.refs_4_, bf16[384,1024]{1,0:T(8,128)(2,1)} %collective-permute-done.1.refs_1_.refs_5_, bf16[384,1024]{1,0:T(8,128)(2,1)} %collective-permute-done.2.refs_2_.refs_6_, bf16[384,1024]{1,0:T(8,128)(2,1)} %collective-permute-done.3.refs_3_.refs_7_, ...), custom_call_target="tpu_custom_call" | custom-call | flops 805306368 | bytes 2097152 | tf_op jit(solution)/shard_map/projected/pallas_call | solution.py:108
  46.9 0.0 copy-done
  46.9 0.0 copy-start.1
  46.9 0.0 copy-start.2
  46.9 0.1 collective-permute-start.4
  47.0 0.0 copy-done.3
  47.0 1.0 fusion.11
  48.0 0.7 collective-permute-done.4
  48.7 0.1 add_convert_fusion.refs_0_
  48.7 3.7 %collective-permute-start.6 = (bf16[384,256]{1,0:T(8,128)(2,1)S(1)}, bf16[384,256]{1,0:T(8,128)(2,1)S(1)}, u32[]{:S(2)}, u32[]{:S(2)}) collective-permute-start(bf16[384,256]{1,0:T(8,128)(2,1)S(1)} %add_convert_fusion.refs_0_), channel_id=1, source_target_pairs={{0,4},{1,5},{2,6},{3,7},{4,8},{5,9},{6,10},{7,11},{8,12},{9,13},{1... | collective-permute-start | bytes 589832 | tf_op jit(solution)/shard_map/ppermute | solution.py:279
  52.5 1.9 %collective-permute-start.5 = (bf16[384,256]{1,0:T(8,128)(2,1)S(1)}, bf16[384,256]{1,0:T(8,128)(2,1)S(1)}, u32[]{:S(2)}, u32[]{:S(2)}) collective-permute-start(bf16[384,256]{1,0:T(8,128)(2,1)S(1)} %add_convert_fusion.refs_0_), channel_id=1, source_target_pairs={{0,2},{1,3},{2,4},{3,5},{4,6},{5,7},{6,8},{7,9},{8,10},{9,11},{10,... | collective-permute-start | bytes 589832 | tf_op jit(solution)/shard_map/ppermute | solution.py:279
  54.3 0.1 collective-permute-start.7
  54.4 3.3 %collective-permute-done.6.refs_2_ = bf16[384,256]{1,0:T(8,128)(2,1)S(1)} collective-permute-done((bf16[384,256]{1,0:T(8,128)(2,1)S(1)}, bf16[384,256]{1,0:T(8,128)(2,1)S(1)}, u32[]{:S(2)}, u32[]{:S(2)}) %collective-permute-start.6) | collective-permute-done | bytes 196640 | tf_op jit(solution)/shard_map/ppermute | solution.py:279
  57.7 0.0 collective-permute-start.9
  57.7 3.4 %collective-permute-done.5.refs_1_ = bf16[384,256]{1,0:T(8,128)(2,1)S(1)} collective-permute-done((bf16[384,256]{1,0:T(8,128)(2,1)S(1)}, bf16[384,256]{1,0:T(8,128)(2,1)S(1)}, u32[]{:S(2)}, u32[]{:S(2)}) %collective-permute-start.5) | collective-permute-done | bytes 196640 | tf_op jit(solution)/shard_map/ppermute | solution.py:279
  61.1 0.0 collective-permute-start.8
  61.1 0.0 collective-permute-done.7.refs_3_
  61.1 0.0 collective-permute-done.9.refs_5_
  61.1 1.4 collective-permute-done.8.refs_4_
  62.6 0.0 copy-done.1
  62.6 0.0 copy-done.2
  62.6 21.4 %attention.1 = (bf16[384,1024]{1,0:T(8,128)(2,1)}, bf16[384,1024]{1,0:T(8,128)(2,1)}, bf16[2,384,256]{2,1,0:T(8,128)(2,1)S(1)}, bf16[3,384,256]{2,1,0:T(8,128)(2,1)S(1)}) custom-call(s32[2]{0:T(128)S(1)} %pad_add_fusion.place_ref, s32[1,264]{1,0:T(1,128)S(1)} %broadcast_in_dim.8.ends_ref, bf16[384,1024]{1,0:T(8,128)(2,1)S(1)} %copy-done.1, ...), custom_call_target="tpu_custom_call" | custom-call | flops 18119393280 | bytes 3932160 | tf_op jit(solution)/shard_map/attention/pallas_call | solution.py:241
  84.0 0.2 collective-permute-start.10
  84.2 1.6 %collective-permute-done.10 = bf16[2,384,256]{2,1,0:T(8,128)(2,1)S(1)} collective-permute-done((bf16[2,384,256]{2,1,0:T(8,128)(2,1)S(1)}, bf16[2,384,256]{2,1,0:T(8,128)(2,1)S(1)}, u32[]{:S(2)}, u32[]{:S(2)}) %collective-permute-start.10) | collective-permute-done | bytes 393248 | tf_op jit(solution)/shard_map/ppermute | solution.py:273
  85.8 0.2 fusion.6
  85.9 1.3 collective-permute-start.12
  87.2 1.3 collective-permute-start.11
  88.5 0.2 collective-permute-start.13
  88.8 8.3 %collective-permute-done.12.refs_10_ = bf16[384,256]{1,0:T(8,128)(2,1)S(1)} collective-permute-done((bf16[384,256]{1,0:T(8,128)(2,1)S(1)}, bf16[384,256]{1,0:T(8,128)(2,1)S(1)}, u32[]{:S(2)}, u32[]{:S(2)}) %collective-permute-start.12) | collective-permute-done | bytes 196640 | tf_op jit(solution)/shard_map/ppermute | solution.py:279
  97.0 0.0 collective-permute-start.15
  97.0 4.0 %collective-permute-done.11.refs_9_ = bf16[384,256]{1,0:T(8,128)(2,1)S(1)} collective-permute-done((bf16[384,256]{1,0:T(8,128)(2,1)S(1)}, bf16[384,256]{1,0:T(8,128)(2,1)S(1)}, u32[]{:S(2)}, u32[]{:S(2)}) %collective-permute-start.11) | collective-permute-done | bytes 196640 | tf_op jit(solution)/shard_map/ppermute | solution.py:279
  101.0 0.0 collective-permute-start.14
  101.0 0.0 collective-permute-done.15.refs_13_
  101.0 1.4 collective-permute-done.14.refs_12_
  102.5 0.0 collective-permute-done.13.refs_11_
  102.5 5.6 %chip_share.1 = bf16[4,1024,256]{2,1,0:T(8,128)(2,1)} custom-call(bf16[384,4096]{1,0:T(8,128)(2,1)} %picked_columns.5.refs_0_.refs_1_.refs_2_.refs_3_, bf16[384,4096]{1,0:T(8,128)(2,1)} %picked_columns.5.refs_0_.refs_1_.refs_2_.refs_3_, bf16[384,4096]{1,0:T(8,128)(2,1)} %picked_columns.5.refs_0_.refs_1_.refs_2_.refs_3_, ...), custom_call_target="tpu_custom_call" | custom-call | flops 1610612736 | bytes 9437184 | tf_op jit(solution)/shard_map/chip_share/pallas_call | solution.py:91
  108.1 40.1 %all_to_all.10 = bf16[64,64,256]{2,1,0:T(8,128)(2,1)S(1)} all-to-all(bf16[64,64,256]{2,1,0:T(8,128)(2,1)} %bitcast.19), channel_id=1, replica_groups=mesh['z'=4,'x'=4,'y'=4,'core'=2] {'z','x','y'}, dimensions={0} | all-to-all | bytes 4194304 | tf_op jit(solution)/shard_map/all_to_all | solution.py:322
  148.2 0.9 convert_reduce_fusion
  (6 shorter events, 0.1 us)
Async XLA Ops:
  3.0 41.1 %all-to-all-start = ((bf16[64,64,256]{2,1,0:T(8,128)(2,1)}), bf16[64,64,256]{2,1,0:T(8,128)(2,1)S(1)}, u32[]{:S(2)}, u32[]{:S(2)}) async-start(bf16[64,64,256]{2,1,0:T(8,128)(2,1)} %broadcast_in_dim.9), calls=%async_computation | async-start | bytes 4194304 | tf_op jit(solution)/shard_map/all_to_all | solution.py:306
  17.8 18.6 %collective-permute-start = (bf16[384,1024]{1,0:T(8,128)(2,1)}, bf16[384,1024]{1,0:T(8,128)(2,1)S(1)}, u32[]{:S(2)}, u32[]{:S(2)}) collective-permute-start(bf16[384,1024]{1,0:T(8,128)(2,1)} %picked_columns.6), channel_id=1, source_target_pairs={{0,1},{1,0},{2,3},{3,2},{4,5},{5,4},{6,7},{7,6},{8,9},{9,8},{10,11... | collective-permute-start | bytes 2359304 | tf_op jit(solution)/shard_map/ppermute | solution.py:273
  20.5 16.0 %collective-permute-start.1 = (bf16[384,1024]{1,0:T(8,128)(2,1)}, bf16[384,1024]{1,0:T(8,128)(2,1)}, u32[]{:S(2)}, u32[]{:S(2)}) collective-permute-start(bf16[384,1024]{1,0:T(8,128)(2,1)} %picked_columns.7), channel_id=1, source_target_pairs={{0,1},{1,0},{2,3},{3,2},{4,5},{5,4},{6,7},{7,6},{8,9},{9,8},{10,11... | collective-permute-start | bytes 2359304 | tf_op jit(solution)/shard_map/ppermute | solution.py:273
  23.7 3.2 %copy-start.4 = (s32[264]{0:T(512)S(1)}, s32[264]{0:T(512)}, u32[]{:S(2)}) copy-start(s32[264]{0:T(512)} %param.9) | copy-start | bytes 3172
  23.7 12.8 %collective-permute-start.2 = (bf16[384,1024]{1,0:T(8,128)(2,1)}, bf16[384,1024]{1,0:T(8,128)(2,1)}, u32[]{:S(2)}, u32[]{:S(2)}) collective-permute-start(bf16[384,1024]{1,0:T(8,128)(2,1)} %picked_columns.8), channel_id=1, source_target_pairs={{0,1},{1,0},{2,3},{3,2},{4,5},{5,4},{6,7},{7,6},{8,9},{9,8},{10,11... | collective-permute-start | bytes 2359304 | tf_op jit(solution)/shard_map/ppermute | solution.py:273
  26.4 10.1 %collective-permute-start.3 = (bf16[384,1024]{1,0:T(8,128)(2,1)}, bf16[384,1024]{1,0:T(8,128)(2,1)}, u32[]{:S(2)}, u32[]{:S(2)}) collective-permute-start(bf16[384,1024]{1,0:T(8,128)(2,1)} %picked_columns.9), channel_id=1, source_target_pairs={{0,1},{1,0},{2,3},{3,2},{4,5},{5,4},{6,7},{7,6},{8,9},{9,8},{10,11... | collective-permute-start | bytes 2359304 | tf_op jit(solution)/shard_map/ppermute | solution.py:273
  36.4 10.4 %copy-start = (bf16[384,1024]{1,0:T(8,128)(2,1)}, bf16[384,1024]{1,0:T(8,128)(2,1)S(1)}, u32[]{:S(2)}) copy-start(bf16[384,1024]{1,0:T(8,128)(2,1)S(1)} %collective-permute-done.refs_0_.refs_4_) | copy-start | bytes 2359300
  44.1 2.9 %copy-start.3 = (bf16[384,4096]{1,0:T(8,128)(2,1)S(1)}, bf16[384,4096]{1,0:T(8,128)(2,1)}, u32[]{:S(2)}) copy-start(bf16[384,4096]{1,0:T(8,128)(2,1)} %picked_columns.5.refs_0_.refs_1_.refs_2_.refs_3_) | copy-start | bytes 9437188
  46.9 15.7 %copy-start.1 = (bf16[384,1024]{1,0:T(8,128)(2,1)S(1)}, bf16[384,1024]{1,0:T(8,128)(2,1)}, u32[]{:S(2)}) copy-start(bf16[384,1024]{1,0:T(8,128)(2,1)} %q_hbm.1) | copy-start | bytes 2359300
  46.9 15.7 %copy-start.2 = (bf16[384,1024]{1,0:T(8,128)(2,1)S(1)}, bf16[384,1024]{1,0:T(8,128)(2,1)}, u32[]{:S(2)}) copy-start(bf16[384,1024]{1,0:T(8,128)(2,1)} %g_hbm.1) | copy-start | bytes 2359300
  46.9 1.8 %collective-permute-start.4 = (f32[384,256]{1,0:T(8,128)S(1)}, f32[384,256]{1,0:T(8,128)S(1)}, u32[]{:S(2)}, u32[]{:S(2)}) collective-permute-start(f32[384,256]{1,0:T(8,128)S(1)} %projected.1), channel_id=1, source_target_pairs={{0,1},{1,0},{2,3},{3,2},{4,5},{5,4},{6,7},{7,6},{8,9},{9,8},{10,11... | collective-permute-start | bytes 1179656 | tf_op jit(solution)/shard_map/ppermute | solution.py:273
  48.7 9.0 %collective-permute-start.6 = (bf16[384,256]{1,0:T(8,128)(2,1)S(1)}, bf16[384,256]{1,0:T(8,128)(2,1)S(1)}, u32[]{:S(2)}, u32[]{:S(2)}) collective-permute-start(bf16[384,256]{1,0:T(8,128)(2,1)S(1)} %add_convert_fusion.refs_0_), channel_id=1, source_target_pairs={{0,4},{1,5},{2,6},{3,7},{4,8},{5,9},{6,10},{7,11},{8,12},{9,13},{1... | collective-permute-start | bytes 589832 | tf_op jit(solution)/shard_map/ppermute | solution.py:279
  52.5 8.7 %collective-permute-start.5 = (bf16[384,256]{1,0:T(8,128)(2,1)S(1)}, bf16[384,256]{1,0:T(8,128)(2,1)S(1)}, u32[]{:S(2)}, u32[]{:S(2)}) collective-permute-start(bf16[384,256]{1,0:T(8,128)(2,1)S(1)} %add_convert_fusion.refs_0_), channel_id=1, source_target_pairs={{0,2},{1,3},{2,4},{3,5},{4,6},{5,7},{6,8},{7,9},{8,10},{9,11},{10,... | collective-permute-start | bytes 589832 | tf_op jit(solution)/shard_map/ppermute | solution.py:279
  54.3 6.8 %collective-permute-start.7 = (bf16[384,256]{1,0:T(8,128)(2,1)S(1)}, bf16[384,256]{1,0:T(8,128)(2,1)S(1)}, u32[]{:S(2)}, u32[]{:S(2)}) collective-permute-start(bf16[384,256]{1,0:T(8,128)(2,1)S(1)} %add_convert_fusion.refs_0_), channel_id=1, source_target_pairs={{0,1},{1,0},{2,3},{3,2},{4,5},{5,4},{6,7},{7,6},{8,9},{9,8},{10,11... | collective-permute-start | bytes 589832 | tf_op jit(solution)/shard_map/ppermute | solution.py:273
  57.7 3.4 %collective-permute-start.9 = (bf16[384,256]{1,0:T(8,128)(2,1)S(1)}, bf16[384,256]{1,0:T(8,128)(2,1)S(1)}, u32[]{:S(2)}, u32[]{:S(2)}) collective-permute-start(bf16[384,256]{1,0:T(8,128)(2,1)S(1)} %collective-permute-done.6.refs_2_), channel_id=1, source_target_pairs={{0,1},{1,0},{2,3},{3,2},{4,5},{5,4},{6,7},{7,6},{8,9},{9,8},{10,11... | collective-permute-start | bytes 589832 | tf_op jit(solution)/shard_map/ppermute | solution.py:273
  61.1 1.4 collective-permute-start.8
  84.0 1.8 %collective-permute-start.10 = (bf16[2,384,256]{2,1,0:T(8,128)(2,1)S(1)}, bf16[2,384,256]{2,1,0:T(8,128)(2,1)S(1)}, u32[]{:S(2)}, u32[]{:S(2)}) collective-permute-start(bf16[2,384,256]{2,1,0:T(8,128)(2,1)S(1)} %get-tuple-element.16), channel_id=1, source_target_pairs={{0,1},{1,0},{2,3},{3,2},{4,5},{5,4},{6,7},{7,6},{8,9},{9,8},{10,11... | collective-permute-start | bytes 1179656 | tf_op jit(solution)/shard_map/ppermute | solution.py:273
  85.9 11.1 %collective-permute-start.12 = (bf16[384,256]{1,0:T(8,128)(2,1)S(1)}, bf16[384,256]{1,0:T(8,128)(2,1)S(1)}, u32[]{:S(2)}, u32[]{:S(2)}) collective-permute-start(bf16[384,256]{1,0:T(8,128)(2,1)S(1)} %get-tuple-element.17), channel_id=1, source_target_pairs={{4,0},{5,1},{6,2},{7,3},{8,4},{9,5},{10,6},{11,7},{12,8},{13,9},{1... | collective-permute-start | bytes 589832 | tf_op jit(solution)/shard_map/ppermute | solution.py:279
  87.2 13.8 %collective-permute-start.11 = (bf16[384,256]{1,0:T(8,128)(2,1)S(1)}, bf16[384,256]{1,0:T(8,128)(2,1)S(1)}, u32[]{:S(2)}, u32[]{:S(2)}) collective-permute-start(bf16[384,256]{1,0:T(8,128)(2,1)S(1)} %get-tuple-element.18), channel_id=1, source_target_pairs={{2,0},{3,1},{4,2},{5,3},{6,4},{7,5},{8,6},{9,7},{10,8},{11,9},{12,... | collective-permute-start | bytes 589832 | tf_op jit(solution)/shard_map/ppermute | solution.py:279
  88.5 13.9 %collective-permute-start.13 = (f32[384,256]{1,0:T(8,128)S(1)}, f32[384,256]{1,0:T(8,128)S(1)}, u32[]{:S(2)}, u32[]{:S(2)}) collective-permute-start(f32[384,256]{1,0:T(8,128)S(1)} %get-tuple-element.19.refs_8_), channel_id=1, source_target_pairs={{0,1},{1,0},{2,3},{3,2},{4,5},{5,4},{6,7},{7,6},{8,9},{9,8},{10,11... | collective-permute-start | bytes 1179656 | tf_op jit(solution)/shard_map/ppermute | solution.py:273
  97.0 4.0 %collective-permute-start.15 = (bf16[384,256]{1,0:T(8,128)(2,1)S(1)}, bf16[384,256]{1,0:T(8,128)(2,1)S(1)}, u32[]{:S(2)}, u32[]{:S(2)}) collective-permute-start(bf16[384,256]{1,0:T(8,128)(2,1)S(1)} %collective-permute-done.12.refs_10_), channel_id=1, source_target_pairs={{0,1},{1,0},{2,3},{3,2},{4,5},{5,4},{6,7},{7,6},{8,9},{9,8},{10,11... | collective-permute-start | bytes 589832 | tf_op jit(solution)/shard_map/ppermute | solution.py:273
  101.0 1.4 collective-permute-start.14

commit v4 on v3

--- a/solution.py
+++ b/solution.py
@@ -98,7 +98,7 @@
         out_shape=jax.ShapeDtypeStruct((chunks, steps * block, pair), BF),
         scratch_shapes=[pltpu.VMEM((rows, pair), BF), pltpu.VMEM((rows, pair), BF)],
         cost_estimate=pl.CostEstimate(flops=4 * width * rows * pair, bytes_accessed=6 * width * rows, transcendentals=0),
-        compiler_params=params(52),
+        compiler_params=params(47),
         name="chip_share",
     )(*([keep] * chunks), *came, *terms)
 
@@ -119,7 +119,7 @@
     chunks = [(0, edge, 0, edge)]
     at = edge
     while at < span - edge:
-        end = min(at + 768, span - edge)
+        end = min(at + 1024, span - edge)
         chunks.append((at, end, 0, rows))
         at = end
     chunks.append((span - edge, span, rows - edge, rows))

time: 150 us -> 149 us (level)
  no operation moved by 1% of the time
where the time goes in v4:
time: 149 us; the launch traced here: 148 us
  Pallas kernels  47.6 us (32%)
  blocking collectives  39.9 us (27%)
  waiting for transfers between devices  31.9 us (21%)
  starting transfers between devices  21.3 us (14%)
  other arithmetic  2.96 us (2%)
  local copies, waits for them, and re-layouts  2.59 us (2%)
    all_to_all x1, blocking collectives, per_device(): spread = lax.all_to_all(share, CHIPS, 0, 0, tiled=True)  39.9 us
    pallas_call x1, Pallas kernels, attention(): pl.pallas_call(attention_kernel, in_specs=[pl.BlockSpec(memory_space=pltp...  21.5 us
    ppermute x4, waiting for transfers between devices, between_chips(): return lax.ppermute(block, ALL, route)  18.9 us
    pallas_call x5, Pallas kernels, picked_columns(): pl.pallas_call(pick_kernel, grid=(steps,), in_specs=[pl.BlockSpec((256, 1...  18.8 us
    all_to_all x1, starting transfers between devices, per_device(): lax.all_to_all(copies, CHIPS, 0, 0, tiled=True).reshape(chips * part, pair)  11.5 us
    ppermute x4, starting transfers between devices, between_chips(): return lax.ppermute(block, ALL, route)  8.17 us
    all_to_all x1, waiting for transfers between devices, per_device(): lax.all_to_all(copies, CHIPS, 0, 0, tiled=True).reshape(chips * part, pair)  7.75 us
    ppermute x12, waiting for transfers between devices, between_cores(): return lax.ppermute(block, 'core', SWAP)  5.16 us
  transfers between devices with their start and end apart: 17, of which 9 were waited for; matrix products, arithmetic and copies ran while one was open for 2% of the time, Pallas kernels for 13%

profile of v4, /device:TPU:0, one launch (start us, length us, event | category | flops | bytes accessed | tf_op | source)
XLA Modules:
  0.0 148.1 jit_solution(7938076718612140910)
XLA Ops:
  0.6 2.4 %broadcast_in_dim.9 = bf16[64,64,256]{2,1,0:T(8,128)(2,1)} broadcast(bf16[64,256]{1,0:T(8,128)(2,1)} %param.6), dimensions={1,2} | broadcast | bytes 2129920 | tf_op jit(solution)/shard_map/broadcast_in_dim | solution.py:305
  3.0 11.5 %all-to-all-start = ((bf16[64,64,256]{2,1,0:T(8,128)(2,1)}), bf16[64,64,256]{2,1,0:T(8,128)(2,1)S(1)}, u32[]{:S(2)}, u32[]{:S(2)}) async-start(bf16[64,64,256]{2,1,0:T(8,128)(2,1)} %broadcast_in_dim.9), calls=%async_computation | async-start | bytes 4194304 | tf_op jit(solution)/shard_map/all_to_all | solution.py:306
  14.5 0.7 fusion.9.pick_ref
  15.2 2.6 %picked_columns.6 = bf16[384,1024]{1,0:T(8,128)(2,1)} custom-call(bf16[256,128]{1,0:T(8,128)(2,1)} %fusion.9.pick_ref, bf16[384,8192]{1,0:T(8,128)(2,1)} %x_ref.9), custom_call_target="tpu_custom_call" | custom-call | bytes 2359296 | tf_op jit(solution)/shard_map/picked_columns/pallas_call | solution.py:70
  17.8 0.0 collective-permute-start
  17.8 2.7 %picked_columns.7 = bf16[384,1024]{1,0:T(8,128)(2,1)} custom-call(bf16[256,128]{1,0:T(8,128)(2,1)} %fusion.9.pick_ref, bf16[384,8192]{1,0:T(8,128)(2,1)} %x_ref.9), custom_call_target="tpu_custom_call" | custom-call | bytes 2359296 | tf_op jit(solution)/shard_map/picked_columns/pallas_call | solution.py:70
  20.5 0.5 collective-permute-start.1
  21.0 2.7 %picked_columns.8 = bf16[384,1024]{1,0:T(8,128)(2,1)} custom-call(bf16[256,128]{1,0:T(8,128)(2,1)} %fusion.9.pick_ref, bf16[384,8192]{1,0:T(8,128)(2,1)} %x_ref.9), custom_call_target="tpu_custom_call" | custom-call | bytes 2359296 | tf_op jit(solution)/shard_map/picked_columns/pallas_call | solution.py:70
  23.7 0.0 copy-start.3
  23.7 0.0 collective-permute-start.2
  23.7 2.7 %picked_columns.9 = bf16[384,1024]{1,0:T(8,128)(2,1)} custom-call(bf16[256,128]{1,0:T(8,128)(2,1)} %fusion.9.pick_ref, bf16[384,8192]{1,0:T(8,128)(2,1)} %x_ref.9), custom_call_target="tpu_custom_call" | custom-call | bytes 2359296 | tf_op jit(solution)/shard_map/picked_columns/pallas_call | solution.py:70
  26.4 0.5 collective-permute-start.3
  26.9 0.0 copy-done.3
  26.9 0.3 reduce-window.9
  27.2 0.1 slice.25
  27.3 0.1 slice_reduce_fusion
  27.4 0.1 add_bitcast_fusion
  27.5 0.7 fusion.8.pick_ref
  28.2 8.1 %picked_columns.5.refs_0_.refs_1_.refs_2_.refs_3_ = bf16[384,4096]{1,0:T(8,128)(2,1)} custom-call(bf16[256,128]{1,0:T(8,128)(2,1)} %fusion.8.pick_ref, bf16[384,8192]{1,0:T(8,128)(2,1)} %x_ref.9), custom_call_target="tpu_custom_call" | custom-call | bytes 9437184 | tf_op jit(solution)/shard_map/picked_columns/pallas_call | solution.py:70
  36.3 0.1 pad_add_fusion.place_ref
  36.3 0.0 collective-permute-done.refs_0_.refs_4_
  36.3 0.0 collective-permute-done.1.refs_1_.refs_5_
  36.3 0.0 collective-permute-done.2.refs_2_.refs_6_
  36.4 0.0 collective-permute-done.3.refs_3_.refs_7_
  36.4 7.7 %all-to-all-done = bf16[64,64,256]{2,1,0:T(8,128)(2,1)S(1)} async-done(((bf16[64,64,256]{2,1,0:T(8,128)(2,1)}), bf16[64,64,256]{2,1,0:T(8,128)(2,1)S(1)}, u32[]{:S(2)}, u32[]{:S(2)}) %all-to-all-start) | async-done | bytes 2097184 | tf_op jit(solution)/shard_map/all_to_all | solution.py:306
  44.1 0.0 copy-start.2
  44.1 2.7 %projected.1 = f32[384,256]{1,0:T(8,128)S(1)} custom-call(bf16[384,1024]{1,0:T(8,128)(2,1)S(1)} %collective-permute-done.refs_0_.refs_4_, bf16[384,1024]{1,0:T(8,128)(2,1)} %collective-permute-done.1.refs_1_.refs_5_, bf16[384,1024]{1,0:T(8,128)(2,1)} %collective-permute-done.2.refs_2_.refs_6_, bf16[384,1024]{1,0:T(8,128)(2,1)} %collective-permute-done.3.refs_3_.refs_7_, ...), custom_call_target="tpu_custom_call" | custom-call | flops 805306368 | bytes 2097152 | tf_op jit(solution)/shard_map/projected/pallas_call | solution.py:108
  46.9 0.0 copy-start
  46.9 0.0 copy-start.1
  46.9 0.1 collective-permute-start.4
  47.0 0.0 copy-done.2
  47.0 1.0 fusion.11
  48.0 0.7 collective-permute-done.4
  48.7 0.1 add_convert_fusion.refs_0_
  48.7 3.7 %collective-permute-start.6 = (bf16[384,256]{1,0:T(8,128)(2,1)S(1)}, bf16[384,256]{1,0:T(8,128)(2,1)S(1)}, u32[]{:S(2)}, u32[]{:S(2)}) collective-permute-start(bf16[384,256]{1,0:T(8,128)(2,1)S(1)} %add_convert_fusion.refs_0_), channel_id=1, source_target_pairs={{0,4},{1,5},{2,6},{3,7},{4,8},{5,9},{6,10},{7,11},{8,12},{9,13},{1... | collective-permute-start | bytes 589832 | tf_op jit(solution)/shard_map/ppermute | solution.py:279
  52.5 1.9 %collective-permute-start.5 = (bf16[384,256]{1,0:T(8,128)(2,1)S(1)}, bf16[384,256]{1,0:T(8,128)(2,1)S(1)}, u32[]{:S(2)}, u32[]{:S(2)}) collective-permute-start(bf16[384,256]{1,0:T(8,128)(2,1)S(1)} %add_convert_fusion.refs_0_), channel_id=1, source_target_pairs={{0,2},{1,3},{2,4},{3,5},{4,6},{5,7},{6,8},{7,9},{8,10},{9,11},{10,... | collective-permute-start | bytes 589832 | tf_op jit(solution)/shard_map/ppermute | solution.py:279
  54.3 0.1 collective-permute-start.7
  54.4 3.3 %collective-permute-done.6.refs_2_ = bf16[384,256]{1,0:T(8,128)(2,1)S(1)} collective-permute-done((bf16[384,256]{1,0:T(8,128)(2,1)S(1)}, bf16[384,256]{1,0:T(8,128)(2,1)S(1)}, u32[]{:S(2)}, u32[]{:S(2)}) %collective-permute-start.6) | collective-permute-done | bytes 196640 | tf_op jit(solution)/shard_map/ppermute | solution.py:279
  57.7 0.0 collective-permute-start.9
  57.7 3.4 %collective-permute-done.5.refs_1_ = bf16[384,256]{1,0:T(8,128)(2,1)S(1)} collective-permute-done((bf16[384,256]{1,0:T(8,128)(2,1)S(1)}, bf16[384,256]{1,0:T(8,128)(2,1)S(1)}, u32[]{:S(2)}, u32[]{:S(2)}) %collective-permute-start.5) | collective-permute-done | bytes 196640 | tf_op jit(solution)/shard_map/ppermute | solution.py:279
  61.1 0.0 collective-permute-start.8
  61.1 0.0 collective-permute-done.7.refs_3_
  61.1 0.0 collective-permute-done.9.refs_5_
  61.1 1.4 collective-permute-done.8.refs_4_
  62.5 0.0 copy-done
  62.5 0.0 copy-done.1
  62.5 21.5 %attention.1 = (bf16[384,1024]{1,0:T(8,128)(2,1)}, bf16[384,1024]{1,0:T(8,128)(2,1)}, bf16[2,384,256]{2,1,0:T(8,128)(2,1)S(1)}, bf16[3,384,256]{2,1,0:T(8,128)(2,1)S(1)}) custom-call(s32[2]{0:T(128)S(1)} %pad_add_fusion.place_ref, s32[1,264]{1,0:T(1,128)S(1)} %broadcast_in_dim.8.ends_ref, bf16[384,1024]{1,0:T(8,128)(2,1)S(1)} %copy-done, ...), custom_call_target="tpu_custom_call" | custom-call | flops 18119393280 | bytes 3932160 | tf_op jit(solution)/shard_map/attention/pallas_call | solution.py:241
  84.0 0.2 collective-permute-start.10
  84.2 1.6 %collective-permute-done.10 = bf16[2,384,256]{2,1,0:T(8,128)(2,1)S(1)} collective-permute-done((bf16[2,384,256]{2,1,0:T(8,128)(2,1)S(1)}, bf16[2,384,256]{2,1,0:T(8,128)(2,1)S(1)}, u32[]{:S(2)}, u32[]{:S(2)}) %collective-permute-start.10) | collective-permute-done | bytes 393248 | tf_op jit(solution)/shard_map/ppermute | solution.py:273
  85.8 0.2 fusion.6
  86.0 1.3 collective-permute-start.12
  87.3 1.3 collective-permute-start.11
  88.6 0.2 collective-permute-start.13
  88.8 8.3 %collective-permute-done.12.refs_10_ = bf16[384,256]{1,0:T(8,128)(2,1)S(1)} collective-permute-done((bf16[384,256]{1,0:T(8,128)(2,1)S(1)}, bf16[384,256]{1,0:T(8,128)(2,1)S(1)}, u32[]{:S(2)}, u32[]{:S(2)}) %collective-permute-start.12) | collective-permute-done | bytes 196640 | tf_op jit(solution)/shard_map/ppermute | solution.py:279
  97.1 0.0 collective-permute-start.15
  97.1 4.0 %collective-permute-done.11.refs_9_ = bf16[384,256]{1,0:T(8,128)(2,1)S(1)} collective-permute-done((bf16[384,256]{1,0:T(8,128)(2,1)S(1)}, bf16[384,256]{1,0:T(8,128)(2,1)S(1)}, u32[]{:S(2)}, u32[]{:S(2)}) %collective-permute-start.11) | collective-permute-done | bytes 196640 | tf_op jit(solution)/shard_map/ppermute | solution.py:279
  101.1 0.0 collective-permute-start.14
  101.1 0.0 collective-permute-done.15.refs_13_
  101.1 1.4 collective-permute-done.14.refs_12_
  102.5 0.0 collective-permute-done.13.refs_11_
  102.5 4.7 %chip_share.1 = bf16[4,1024,256]{2,1,0:T(8,128)(2,1)S(1)} custom-call(bf16[384,4096]{1,0:T(8,128)(2,1)} %picked_columns.5.refs_0_.refs_1_.refs_2_.refs_3_, bf16[384,4096]{1,0:T(8,128)(2,1)} %picked_columns.5.refs_0_.refs_1_.refs_2_.refs_3_, bf16[384,4096]{1,0:T(8,128)(2,1)} %picked_columns.5.refs_0_.refs_1_.refs_2_.refs_3_, ...), custom_call_target="tpu_custom_call" | custom-call | flops 1610612736 | bytes 9437184 | tf_op jit(solution)/shard_map/chip_share/pallas_call | solution.py:91
  107.2 39.9 %all_to_all.10 = bf16[64,64,256]{2,1,0:T(8,128)(2,1)S(1)} all-to-all(bf16[64,64,256]{2,1,0:T(8,128)(2,1)S(1)} %bitcast.17), channel_id=1, replica_groups=mesh['z'=4,'x'=4,'y'=4,'core'=2] {'z','x','y'}, dimensions={0} | all-to-all | bytes 4194304 | tf_op jit(solution)/shard_map/all_to_all | solution.py:322
  147.1 0.9 convert_reduce_fusion
  (5 shorter events, 0.1 us)
Async XLA Ops:
  3.0 41.1 %all-to-all-start = ((bf16[64,64,256]{2,1,0:T(8,128)(2,1)}), bf16[64,64,256]{2,1,0:T(8,128)(2,1)S(1)}, u32[]{:S(2)}, u32[]{:S(2)}) async-start(bf16[64,64,256]{2,1,0:T(8,128)(2,1)} %broadcast_in_dim.9), calls=%async_computation | async-start | bytes 4194304 | tf_op jit(solution)/shard_map/all_to_all | solution.py:306
  17.8 18.5 %collective-permute-start = (bf16[384,1024]{1,0:T(8,128)(2,1)}, bf16[384,1024]{1,0:T(8,128)(2,1)S(1)}, u32[]{:S(2)}, u32[]{:S(2)}) collective-permute-start(bf16[384,1024]{1,0:T(8,128)(2,1)} %picked_columns.6), channel_id=1, source_target_pairs={{0,1},{1,0},{2,3},{3,2},{4,5},{5,4},{6,7},{7,6},{8,9},{9,8},{10,11... | collective-permute-start | bytes 2359304 | tf_op jit(solution)/shard_map/ppermute | solution.py:273
  20.5 15.9 %collective-permute-start.1 = (bf16[384,1024]{1,0:T(8,128)(2,1)}, bf16[384,1024]{1,0:T(8,128)(2,1)}, u32[]{:S(2)}, u32[]{:S(2)}) collective-permute-start(bf16[384,1024]{1,0:T(8,128)(2,1)} %picked_columns.7), channel_id=1, source_target_pairs={{0,1},{1,0},{2,3},{3,2},{4,5},{5,4},{6,7},{7,6},{8,9},{9,8},{10,11... | collective-permute-start | bytes 2359304 | tf_op jit(solution)/shard_map/ppermute | solution.py:273
  23.7 3.2 %copy-start.3 = (s32[264]{0:T(512)S(1)}, s32[264]{0:T(512)}, u32[]{:S(2)}) copy-start(s32[264]{0:T(512)} %param.9) | copy-start | bytes 3172
  23.7 12.7 %collective-permute-start.2 = (bf16[384,1024]{1,0:T(8,128)(2,1)}, bf16[384,1024]{1,0:T(8,128)(2,1)}, u32[]{:S(2)}, u32[]{:S(2)}) collective-permute-start(bf16[384,1024]{1,0:T(8,128)(2,1)} %picked_columns.8), channel_id=1, source_target_pairs={{0,1},{1,0},{2,3},{3,2},{4,5},{5,4},{6,7},{7,6},{8,9},{9,8},{10,11... | collective-permute-start | bytes 2359304 | tf_op jit(solution)/shard_map/ppermute | solution.py:273
  26.4 10.0 %collective-permute-start.3 = (bf16[384,1024]{1,0:T(8,128)(2,1)}, bf16[384,1024]{1,0:T(8,128)(2,1)}, u32[]{:S(2)}, u32[]{:S(2)}) collective-permute-start(bf16[384,1024]{1,0:T(8,128)(2,1)} %picked_columns.9), channel_id=1, source_target_pairs={{0,1},{1,0},{2,3},{3,2},{4,5},{5,4},{6,7},{7,6},{8,9},{9,8},{10,11... | collective-permute-start | bytes 2359304 | tf_op jit(solution)/shard_map/ppermute | solution.py:273
  44.1 2.9 %copy-start.2 = (bf16[384,4096]{1,0:T(8,128)(2,1)S(1)}, bf16[384,4096]{1,0:T(8,128)(2,1)}, u32[]{:S(2)}) copy-start(bf16[384,4096]{1,0:T(8,128)(2,1)} %picked_columns.5.refs_0_.refs_1_.refs_2_.refs_3_) | copy-start | bytes 9437188
  46.9 15.7 %copy-start = (bf16[384,1024]{1,0:T(8,128)(2,1)S(1)}, bf16[384,1024]{1,0:T(8,128)(2,1)}, u32[]{:S(2)}) copy-start(bf16[384,1024]{1,0:T(8,128)(2,1)} %q_hbm.1) | copy-start | bytes 2359300
  46.9 15.7 %copy-start.1 = (bf16[384,1024]{1,0:T(8,128)(2,1)S(1)}, bf16[384,1024]{1,0:T(8,128)(2,1)}, u32[]{:S(2)}) copy-start(bf16[384,1024]{1,0:T(8,128)(2,1)} %g_hbm.1) | copy-start | bytes 2359300
  46.9 1.8 %collective-permute-start.4 = (f32[384,256]{1,0:T(8,128)S(1)}, f32[384,256]{1,0:T(8,128)S(1)}, u32[]{:S(2)}, u32[]{:S(2)}) collective-permute-start(f32[384,256]{1,0:T(8,128)S(1)} %projected.1), channel_id=1, source_target_pairs={{0,1},{1,0},{2,3},{3,2},{4,5},{5,4},{6,7},{7,6},{8,9},{9,8},{10,11... | collective-permute-start | bytes 1179656 | tf_op jit(solution)/shard_map/ppermute | solution.py:273
  48.7 9.0 %collective-permute-start.6 = (bf16[384,256]{1,0:T(8,128)(2,1)S(1)}, bf16[384,256]{1,0:T(8,128)(2,1)S(1)}, u32[]{:S(2)}, u32[]{:S(2)}) collective-permute-start(bf16[384,256]{1,0:T(8,128)(2,1)S(1)} %add_convert_fusion.refs_0_), channel_id=1, source_target_pairs={{0,4},{1,5},{2,6},{3,7},{4,8},{5,9},{6,10},{7,11},{8,12},{9,13},{1... | collective-permute-start | bytes 589832 | tf_op jit(solution)/shard_map/ppermute | solution.py:279
  52.5 8.7 %collective-permute-start.5 = (bf16[384,256]{1,0:T(8,128)(2,1)S(1)}, bf16[384,256]{1,0:T(8,128)(2,1)S(1)}, u32[]{:S(2)}, u32[]{:S(2)}) collective-permute-start(bf16[384,256]{1,0:T(8,128)(2,1)S(1)} %add_convert_fusion.refs_0_), channel_id=1, source_target_pairs={{0,2},{1,3},{2,4},{3,5},{4,6},{5,7},{6,8},{7,9},{8,10},{9,11},{10,... | collective-permute-start | bytes 589832 | tf_op jit(solution)/shard_map/ppermute | solution.py:279
  54.3 6.8 %collective-permute-start.7 = (bf16[384,256]{1,0:T(8,128)(2,1)S(1)}, bf16[384,256]{1,0:T(8,128)(2,1)S(1)}, u32[]{:S(2)}, u32[]{:S(2)}) collective-permute-start(bf16[384,256]{1,0:T(8,128)(2,1)S(1)} %add_convert_fusion.refs_0_), channel_id=1, source_target_pairs={{0,1},{1,0},{2,3},{3,2},{4,5},{5,4},{6,7},{7,6},{8,9},{9,8},{10,11... | collective-permute-start | bytes 589832 | tf_op jit(solution)/shard_map/ppermute | solution.py:273
  57.7 3.4 %collective-permute-start.9 = (bf16[384,256]{1,0:T(8,128)(2,1)S(1)}, bf16[384,256]{1,0:T(8,128)(2,1)S(1)}, u32[]{:S(2)}, u32[]{:S(2)}) collective-permute-start(bf16[384,256]{1,0:T(8,128)(2,1)S(1)} %collective-permute-done.6.refs_2_), channel_id=1, source_target_pairs={{0,1},{1,0},{2,3},{3,2},{4,5},{5,4},{6,7},{7,6},{8,9},{9,8},{10,11... | collective-permute-start | bytes 589832 | tf_op jit(solution)/shard_map/ppermute | solution.py:273
  61.1 1.4 collective-permute-start.8
  84.0 1.8 %collective-permute-start.10 = (bf16[2,384,256]{2,1,0:T(8,128)(2,1)S(1)}, bf16[2,384,256]{2,1,0:T(8,128)(2,1)S(1)}, u32[]{:S(2)}, u32[]{:S(2)}) collective-permute-start(bf16[2,384,256]{2,1,0:T(8,128)(2,1)S(1)} %get-tuple-element.16), channel_id=1, source_target_pairs={{0,1},{1,0},{2,3},{3,2},{4,5},{5,4},{6,7},{7,6},{8,9},{9,8},{10,11... | collective-permute-start | bytes 1179656 | tf_op jit(solution)/shard_map/ppermute | solution.py:273
  86.0 11.1 %collective-permute-start.12 = (bf16[384,256]{1,0:T(8,128)(2,1)S(1)}, bf16[384,256]{1,0:T(8,128)(2,1)S(1)}, u32[]{:S(2)}, u32[]{:S(2)}) collective-permute-start(bf16[384,256]{1,0:T(8,128)(2,1)S(1)} %get-tuple-element.17), channel_id=1, source_target_pairs={{4,0},{5,1},{6,2},{7,3},{8,4},{9,5},{10,6},{11,7},{12,8},{13,9},{1... | collective-permute-start | bytes 589832 | tf_op jit(solution)/shard_map/ppermute | solution.py:279
  87.3 13.8 %collective-permute-start.11 = (bf16[384,256]{1,0:T(8,128)(2,1)S(1)}, bf16[384,256]{1,0:T(8,128)(2,1)S(1)}, u32[]{:S(2)}, u32[]{:S(2)}) collective-permute-start(bf16[384,256]{1,0:T(8,128)(2,1)S(1)} %get-tuple-element.18), channel_id=1, source_target_pairs={{2,0},{3,1},{4,2},{5,3},{6,4},{7,5},{8,6},{9,7},{10,8},{11,9},{12,... | collective-permute-start | bytes 589832 | tf_op jit(solution)/shard_map/ppermute | solution.py:279
  88.6 13.9 %collective-permute-start.13 = (f32[384,256]{1,0:T(8,128)S(1)}, f32[384,256]{1,0:T(8,128)S(1)}, u32[]{:S(2)}, u32[]{:S(2)}) collective-permute-start(f32[384,256]{1,0:T(8,128)S(1)} %get-tuple-element.19.refs_8_), channel_id=1, source_target_pairs={{0,1},{1,0},{2,3},{3,2},{4,5},{5,4},{6,7},{7,6},{8,9},{9,8},{10,11... | collective-permute-start | bytes 1179656 | tf_op jit(solution)/shard_map/ppermute | solution.py:273
  97.1 4.0 %collective-permute-start.15 = (bf16[384,256]{1,0:T(8,128)(2,1)S(1)}, bf16[384,256]{1,0:T(8,128)(2,1)S(1)}, u32[]{:S(2)}, u32[]{:S(2)}) collective-permute-start(bf16[384,256]{1,0:T(8,128)(2,1)S(1)} %collective-permute-done.12.refs_10_), channel_id=1, source_target_pairs={{0,1},{1,0},{2,3},{3,2},{4,5},{5,4},{6,7},{7,6},{8,9},{9,8},{10,11... | collective-permute-start | bytes 589832 | tf_op jit(solution)/shard_map/ppermute | solution.py:273
  101.1 1.4 collective-permute-start.14

commit v5 on v4

--- a/solution.py
+++ b/solution.py
@@ -137,7 +137,7 @@
 
 def attention_kernel(place_ref, ends_ref, q_hbm, g_hbm, *refs):
     pieces = refs[:PIECES]
-    out_hbm, dq_hbm, swap_ref, rest_ref, kv_ref, turned_ref, bias_ref, s_ref, p_ref, acc_ref, *refs = refs[PIECES:]
+    out_hbm, dq_hbm, swap_ref, rest_ref, kv_ref, ones_ref, turned_ref, bias_ref, s_ref, p_ref, acc_ref, *refs = refs[PIECES:]
     q_ref, g_ref, out_ref, dq_ref, sems = refs
     rows = q_ref.shape[0]
     size = kv_ref.shape[1] // 2
@@ -163,6 +163,8 @@
     for j, piece in enumerate([fourth, third, second, first, own]):
         cols = slice(j * rows, (j + 1) * rows)
         kv_ref[cols, :] = piece
+        ones_ref[cols, :size] = piece[:, size:]
+        ones_ref[cols, size:] = jnp.ones((rows, size), BF)
         turned_ref[:size, cols] = piece[:, :size].T
         turned_ref[size:, cols] = piece[:, size:].T
         at = lax.broadcasted_iota(jnp.int32, (rows, rows), 1) + j * rows
@@ -184,17 +186,15 @@
             top = jnp.concatenate([part for part in parts if part.shape[0]], axis=0)
             yield
         peak = jnp.max(top, axis=1, keepdims=True) * scale2
-        total = jnp.zeros((rows, size), F32)
-        out = jnp.zeros((rows, size), F32)
+        out = jnp.zeros((rows, 2 * size), F32)
         for c0, c1, r0, r1 in chunks:
             e = jnp.exp2(s_ref[h % 2, r0:r1, c0:c1] * scale2 - peak[r0:r1])
-            total = onto_rows(total, functools.reduce(jnp.add, lane_groups(e, size)), r0, r1)
             p = e.astype(BF)
             p_ref[h % 2, r0:r1, c0:c1] = p
-            out = onto_rows(out, mm(p, kv_ref[c0:c1, size:]), r0, r1)
+            out = onto_rows(out, mm(p, ones_ref[c0:c1, :]), r0, r1)
             yield
-        inverse = 1.0 / jnp.sum(total, axis=1, keepdims=True)
-        out = out * inverse
+        inverse = 1.0 / out[:, size:]
+        out = out[:, :size] * inverse
         out_ref[:, lanes] = out.astype(BF)
         scaled = g_ref[:, lanes].astype(F32) * inverse
         g = scaled.astype(BF)
@@ -250,6 +250,7 @@
         ],
         scratch_shapes=[
             pltpu.VMEM((span, pair), BF),
+            pltpu.VMEM((span, pair), BF),
             pltpu.VMEM((pair, span), BF),
             pltpu.VMEM((rows, span), F32),
             pltpu.VMEM((2, rows, span), F32),

time: 149 us -> 149 us (level)
  no operation moved by 1% of the time
where the time goes in v5:
time: 149 us
  Pallas kernels  48.3 us (32%)
  blocking collectives  39.9 us (27%)
  waiting for transfers between devices  31.9 us (21%)
  starting transfers between devices  21.3 us (14%)
  other arithmetic  2.96 us (2%)
  local copies, waits for them, and re-layouts  2.59 us (2%)
    all_to_all x1, blocking collectives, per_device(): spread = lax.all_to_all(share, CHIPS, 0, 0, tiled=True)  39.9 us
    pallas_call x1, Pallas kernels, attention(): pl.pallas_call(attention_kernel, in_specs=[pl.BlockSpec(memory_space=pltp...  22.1 us
    ppermute x4, waiting for transfers between devices, between_chips(): return lax.ppermute(block, ALL, route)  18.9 us
    pallas_call x5, Pallas kernels, picked_columns(): pl.pallas_call(pick_kernel, grid=(steps,), in_specs=[pl.BlockSpec((256, 1...  18.8 us
    all_to_all x1, starting transfers between devices, per_device(): lax.all_to_all(copies, CHIPS, 0, 0, tiled=True).reshape(chips * part, pair)  11.5 us
    ppermute x4, starting transfers between devices, between_chips(): return lax.ppermute(block, ALL, route)  8.17 us
    all_to_all x1, waiting for transfers between devices, per_device(): lax.all_to_all(copies, CHIPS, 0, 0, tiled=True).reshape(chips * part, pair)  7.75 us
    ppermute x12, waiting for transfers between devices, between_cores(): return lax.ppermute(block, 'core', SWAP)  5.18 us
  transfers between devices with their start and end apart: 17, of which 9 were waited for; matrix products, arithmetic and copies ran while one was open for 2% of the time, Pallas kernels for 13%

profile of v5, /device:TPU:0, one launch (start us, length us, event | category | flops | bytes accessed | tf_op | source)
XLA Modules:
  0.0 148.7 jit_solution(15853324571787959582)
XLA Ops:
  0.6 2.4 %broadcast_in_dim.9 = bf16[64,64,256]{2,1,0:T(8,128)(2,1)} broadcast(bf16[64,256]{1,0:T(8,128)(2,1)} %param.6), dimensions={1,2} | broadcast | bytes 2129920 | tf_op jit(solution)/shard_map/broadcast_in_dim | solution.py:306
  3.0 11.5 %all-to-all-start = ((bf16[64,64,256]{2,1,0:T(8,128)(2,1)}), bf16[64,64,256]{2,1,0:T(8,128)(2,1)S(1)}, u32[]{:S(2)}, u32[]{:S(2)}) async-start(bf16[64,64,256]{2,1,0:T(8,128)(2,1)} %broadcast_in_dim.9), calls=%async_computation | async-start | bytes 4194304 | tf_op jit(solution)/shard_map/all_to_all | solution.py:307
  14.5 0.7 fusion.9.pick_ref
  15.2 2.6 %picked_columns.6 = bf16[384,1024]{1,0:T(8,128)(2,1)} custom-call(bf16[256,128]{1,0:T(8,128)(2,1)} %fusion.9.pick_ref, bf16[384,8192]{1,0:T(8,128)(2,1)} %x_ref.9), custom_call_target="tpu_custom_call" | custom-call | bytes 2359296 | tf_op jit(solution)/shard_map/picked_columns/pallas_call | solution.py:70
  17.8 0.0 collective-permute-start
  17.8 2.7 %picked_columns.7 = bf16[384,1024]{1,0:T(8,128)(2,1)} custom-call(bf16[256,128]{1,0:T(8,128)(2,1)} %fusion.9.pick_ref, bf16[384,8192]{1,0:T(8,128)(2,1)} %x_ref.9), custom_call_target="tpu_custom_call" | custom-call | bytes 2359296 | tf_op jit(solution)/shard_map/picked_columns/pallas_call | solution.py:70
  20.5 0.5 collective-permute-start.1
  21.0 2.7 %picked_columns.8 = bf16[384,1024]{1,0:T(8,128)(2,1)} custom-call(bf16[256,128]{1,0:T(8,128)(2,1)} %fusion.9.pick_ref, bf16[384,8192]{1,0:T(8,128)(2,1)} %x_ref.9), custom_call_target="tpu_custom_call" | custom-call | bytes 2359296 | tf_op jit(solution)/shard_map/picked_columns/pallas_call | solution.py:70
  23.7 0.0 copy-start.3
  23.7 0.0 collective-permute-start.2
  23.7 2.7 %picked_columns.9 = bf16[384,1024]{1,0:T(8,128)(2,1)} custom-call(bf16[256,128]{1,0:T(8,128)(2,1)} %fusion.9.pick_ref, bf16[384,8192]{1,0:T(8,128)(2,1)} %x_ref.9), custom_call_target="tpu_custom_call" | custom-call | bytes 2359296 | tf_op jit(solution)/shard_map/picked_columns/pallas_call | solution.py:70
  26.4 0.5 collective-permute-start.3
  26.9 0.0 copy-done.3
  26.9 0.3 reduce-window.9
  27.2 0.1 slice.25
  27.3 0.1 slice_reduce_fusion
  27.4 0.1 add_bitcast_fusion
  27.5 0.7 fusion.8.pick_ref
  28.2 8.1 %picked_columns.5.refs_0_.refs_1_.refs_2_.refs_3_ = bf16[384,4096]{1,0:T(8,128)(2,1)} custom-call(bf16[256,128]{1,0:T(8,128)(2,1)} %fusion.8.pick_ref, bf16[384,8192]{1,0:T(8,128)(2,1)} %x_ref.9), custom_call_target="tpu_custom_call" | custom-call | bytes 9437184 | tf_op jit(solution)/shard_map/picked_columns/pallas_call | solution.py:70
  36.3 0.1 pad_add_fusion.place_ref
  36.3 0.0 collective-permute-done.refs_0_.refs_4_
  36.3 0.0 collective-permute-done.1.refs_1_.refs_5_
  36.3 0.0 collective-permute-done.2.refs_2_.refs_6_
  36.4 0.0 collective-permute-done.3.refs_3_.refs_7_
  36.4 7.7 %all-to-all-done = bf16[64,64,256]{2,1,0:T(8,128)(2,1)S(1)} async-done(((bf16[64,64,256]{2,1,0:T(8,128)(2,1)}), bf16[64,64,256]{2,1,0:T(8,128)(2,1)S(1)}, u32[]{:S(2)}, u32[]{:S(2)}) %all-to-all-start) | async-done | bytes 2097184 | tf_op jit(solution)/shard_map/all_to_all | solution.py:307
  44.1 0.0 copy-start.2
  44.1 2.7 %projected.1 = f32[384,256]{1,0:T(8,128)S(1)} custom-call(bf16[384,1024]{1,0:T(8,128)(2,1)S(1)} %collective-permute-done.refs_0_.refs_4_, bf16[384,1024]{1,0:T(8,128)(2,1)} %collective-permute-done.1.refs_1_.refs_5_, bf16[384,1024]{1,0:T(8,128)(2,1)} %collective-permute-done.2.refs_2_.refs_6_, bf16[384,1024]{1,0:T(8,128)(2,1)} %collective-permute-done.3.refs_3_.refs_7_, ...), custom_call_target="tpu_custom_call" | custom-call | flops 805306368 | bytes 2097152 | tf_op jit(solution)/shard_map/projected/pallas_call | solution.py:108
  46.9 0.0 copy-start
  46.9 0.0 copy-start.1
  46.9 0.1 collective-permute-start.4
  47.0 0.0 copy-done.2
  47.0 1.0 fusion.11
  48.0 0.7 collective-permute-done.4
  48.7 0.1 add_convert_fusion.refs_0_
  48.7 3.7 %collective-permute-start.6 = (bf16[384,256]{1,0:T(8,128)(2,1)S(1)}, bf16[384,256]{1,0:T(8,128)(2,1)S(1)}, u32[]{:S(2)}, u32[]{:S(2)}) collective-permute-start(bf16[384,256]{1,0:T(8,128)(2,1)S(1)} %add_convert_fusion.refs_0_), channel_id=1, source_target_pairs={{0,4},{1,5},{2,6},{3,7},{4,8},{5,9},{6,10},{7,11},{8,12},{9,13},{1... | collective-permute-start | bytes 589832 | tf_op jit(solution)/shard_map/ppermute | solution.py:280
  52.5 1.9 %collective-permute-start.5 = (bf16[384,256]{1,0:T(8,128)(2,1)S(1)}, bf16[384,256]{1,0:T(8,128)(2,1)S(1)}, u32[]{:S(2)}, u32[]{:S(2)}) collective-permute-start(bf16[384,256]{1,0:T(8,128)(2,1)S(1)} %add_convert_fusion.refs_0_), channel_id=1, source_target_pairs={{0,2},{1,3},{2,4},{3,5},{4,6},{5,7},{6,8},{7,9},{8,10},{9,11},{10,... | collective-permute-start | bytes 589832 | tf_op jit(solution)/shard_map/ppermute | solution.py:280
  54.3 0.1 collective-permute-start.7
  54.4 3.3 %collective-permute-done.6.refs_2_ = bf16[384,256]{1,0:T(8,128)(2,1)S(1)} collective-permute-done((bf16[384,256]{1,0:T(8,128)(2,1)S(1)}, bf16[384,256]{1,0:T(8,128)(2,1)S(1)}, u32[]{:S(2)}, u32[]{:S(2)}) %collective-permute-start.6) | collective-permute-done | bytes 196640 | tf_op jit(solution)/shard_map/ppermute | solution.py:280
  57.7 0.0 collective-permute-start.9
  57.7 3.4 %collective-permute-done.5.refs_1_ = bf16[384,256]{1,0:T(8,128)(2,1)S(1)} collective-permute-done((bf16[384,256]{1,0:T(8,128)(2,1)S(1)}, bf16[384,256]{1,0:T(8,128)(2,1)S(1)}, u32[]{:S(2)}, u32[]{:S(2)}) %collective-permute-start.5) | collective-permute-done | bytes 196640 | tf_op jit(solution)/shard_map/ppermute | solution.py:280
  61.1 0.0 collective-permute-start.8
  61.1 0.0 collective-permute-done.7.refs_3_
  61.1 0.0 collective-permute-done.9.refs_5_
  61.1 1.4 collective-permute-done.8.refs_4_
  62.5 0.0 copy-done
  62.5 0.0 copy-done.1
  62.5 22.1 %attention.1 = (bf16[384,1024]{1,0:T(8,128)(2,1)}, bf16[384,1024]{1,0:T(8,128)(2,1)}, bf16[2,384,256]{2,1,0:T(8,128)(2,1)S(1)}, bf16[3,384,256]{2,1,0:T(8,128)(2,1)S(1)}) custom-call(s32[2]{0:T(128)S(1)} %pad_add_fusion.place_ref, s32[1,264]{1,0:T(1,128)S(1)} %broadcast_in_dim.8.ends_ref, bf16[384,1024]{1,0:T(8,128)(2,1)S(1)} %copy-done, ...), custom_call_target="tpu_custom_call" | custom-call | flops 18119393280 | bytes 3932160 | tf_op jit(solution)/shard_map/attention/pallas_call | solution.py:241
  84.7 0.2 collective-permute-start.10
  84.9 1.6 %collective-permute-done.10 = bf16[2,384,256]{2,1,0:T(8,128)(2,1)S(1)} collective-permute-done((bf16[2,384,256]{2,1,0:T(8,128)(2,1)S(1)}, bf16[2,384,256]{2,1,0:T(8,128)(2,1)S(1)}, u32[]{:S(2)}, u32[]{:S(2)}) %collective-permute-start.10) | collective-permute-done | bytes 393248 | tf_op jit(solution)/shard_map/ppermute | solution.py:274
  86.5 0.2 fusion.6
  86.6 1.3 collective-permute-start.12
  87.9 1.3 collective-permute-start.11
  89.2 0.2 collective-permute-start.13
  89.5 8.3 %collective-permute-done.12.refs_10_ = bf16[384,256]{1,0:T(8,128)(2,1)S(1)} collective-permute-done((bf16[384,256]{1,0:T(8,128)(2,1)S(1)}, bf16[384,256]{1,0:T(8,128)(2,1)S(1)}, u32[]{:S(2)}, u32[]{:S(2)}) %collective-permute-start.12) | collective-permute-done | bytes 196640 | tf_op jit(solution)/shard_map/ppermute | solution.py:280
  97.7 0.0 collective-permute-start.15
  97.7 4.0 %collective-permute-done.11.refs_9_ = bf16[384,256]{1,0:T(8,128)(2,1)S(1)} collective-permute-done((bf16[384,256]{1,0:T(8,128)(2,1)S(1)}, bf16[384,256]{1,0:T(8,128)(2,1)S(1)}, u32[]{:S(2)}, u32[]{:S(2)}) %collective-permute-start.11) | collective-permute-done | bytes 196640 | tf_op jit(solution)/shard_map/ppermute | solution.py:280
  101.7 0.0 collective-permute-start.14
  101.8 0.0 collective-permute-done.15.refs_13_
  101.8 1.4 collective-permute-done.14.refs_12_
  103.2 0.0 collective-permute-done.13.refs_11_
  103.2 4.7 %chip_share.1 = bf16[4,1024,256]{2,1,0:T(8,128)(2,1)S(1)} custom-call(bf16[384,4096]{1,0:T(8,128)(2,1)} %picked_columns.5.refs_0_.refs_1_.refs_2_.refs_3_, bf16[384,4096]{1,0:T(8,128)(2,1)} %picked_columns.5.refs_0_.refs_1_.refs_2_.refs_3_, bf16[384,4096]{1,0:T(8,128)(2,1)} %picked_columns.5.refs_0_.refs_1_.refs_2_.refs_3_, ...), custom_call_target="tpu_custom_call" | custom-call | flops 1610612736 | bytes 9437184 | tf_op jit(solution)/shard_map/chip_share/pallas_call | solution.py:91
  107.9 39.9 %all_to_all.10 = bf16[64,64,256]{2,1,0:T(8,128)(2,1)S(1)} all-to-all(bf16[64,64,256]{2,1,0:T(8,128)(2,1)S(1)} %bitcast.17), channel_id=1, replica_groups=mesh['z'=4,'x'=4,'y'=4,'core'=2] {'z','x','y'}, dimensions={0} | all-to-all | bytes 4194304 | tf_op jit(solution)/shard_map/all_to_all | solution.py:323
  147.8 0.9 convert_reduce_fusion
  (5 shorter events, 0.1 us)
Async XLA Ops:
  3.0 41.1 %all-to-all-start = ((bf16[64,64,256]{2,1,0:T(8,128)(2,1)}), bf16[64,64,256]{2,1,0:T(8,128)(2,1)S(1)}, u32[]{:S(2)}, u32[]{:S(2)}) async-start(bf16[64,64,256]{2,1,0:T(8,128)(2,1)} %broadcast_in_dim.9), calls=%async_computation | async-start | bytes 4194304 | tf_op jit(solution)/shard_map/all_to_all | solution.py:307
  17.8 18.5 %collective-permute-start = (bf16[384,1024]{1,0:T(8,128)(2,1)}, bf16[384,1024]{1,0:T(8,128)(2,1)S(1)}, u32[]{:S(2)}, u32[]{:S(2)}) collective-permute-start(bf16[384,1024]{1,0:T(8,128)(2,1)} %picked_columns.6), channel_id=1, source_target_pairs={{0,1},{1,0},{2,3},{3,2},{4,5},{5,4},{6,7},{7,6},{8,9},{9,8},{10,11... | collective-permute-start | bytes 2359304 | tf_op jit(solution)/shard_map/ppermute | solution.py:274
  20.5 15.9 %collective-permute-start.1 = (bf16[384,1024]{1,0:T(8,128)(2,1)}, bf16[384,1024]{1,0:T(8,128)(2,1)}, u32[]{:S(2)}, u32[]{:S(2)}) collective-permute-start(bf16[384,1024]{1,0:T(8,128)(2,1)} %picked_columns.7), channel_id=1, source_target_pairs={{0,1},{1,0},{2,3},{3,2},{4,5},{5,4},{6,7},{7,6},{8,9},{9,8},{10,11... | collective-permute-start | bytes 2359304 | tf_op jit(solution)/shard_map/ppermute | solution.py:274
  23.7 3.2 %copy-start.3 = (s32[264]{0:T(512)S(1)}, s32[264]{0:T(512)}, u32[]{:S(2)}) copy-start(s32[264]{0:T(512)} %param.9) | copy-start | bytes 3172
  23.7 12.7 %collective-permute-start.2 = (bf16[384,1024]{1,0:T(8,128)(2,1)}, bf16[384,1024]{1,0:T(8,128)(2,1)}, u32[]{:S(2)}, u32[]{:S(2)}) collective-permute-start(bf16[384,1024]{1,0:T(8,128)(2,1)} %picked_columns.8), channel_id=1, source_target_pairs={{0,1},{1,0},{2,3},{3,2},{4,5},{5,4},{6,7},{7,6},{8,9},{9,8},{10,11... | collective-permute-start | bytes 2359304 | tf_op jit(solution)/shard_map/ppermute | solution.py:274
  26.4 10.0 %collective-permute-start.3 = (bf16[384,1024]{1,0:T(8,128)(2,1)}, bf16[384,1024]{1,0:T(8,128)(2,1)}, u32[]{:S(2)}, u32[]{:S(2)}) collective-permute-start(bf16[384,1024]{1,0:T(8,128)(2,1)} %picked_columns.9), channel_id=1, source_target_pairs={{0,1},{1,0},{2,3},{3,2},{4,5},{5,4},{6,7},{7,6},{8,9},{9,8},{10,11... | collective-permute-start | bytes 2359304 | tf_op jit(solution)/shard_map/ppermute | solution.py:274
  44.1 2.9 %copy-start.2 = (bf16[384,4096]{1,0:T(8,128)(2,1)S(1)}, bf16[384,4096]{1,0:T(8,128)(2,1)}, u32[]{:S(2)}) copy-start(bf16[384,4096]{1,0:T(8,128)(2,1)} %picked_columns.5.refs_0_.refs_1_.refs_2_.refs_3_) | copy-start | bytes 9437188
  46.9 15.7 %copy-start = (bf16[384,1024]{1,0:T(8,128)(2,1)S(1)}, bf16[384,1024]{1,0:T(8,128)(2,1)}, u32[]{:S(2)}) copy-start(bf16[384,1024]{1,0:T(8,128)(2,1)} %q_hbm.1) | copy-start | bytes 2359300
  46.9 15.7 %copy-start.1 = (bf16[384,1024]{1,0:T(8,128)(2,1)S(1)}, bf16[384,1024]{1,0:T(8,128)(2,1)}, u32[]{:S(2)}) copy-start(bf16[384,1024]{1,0:T(8,128)(2,1)} %g_hbm.1) | copy-start | bytes 2359300
  46.9 1.8 %collective-permute-start.4 = (f32[384,256]{1,0:T(8,128)S(1)}, f32[384,256]{1,0:T(8,128)S(1)}, u32[]{:S(2)}, u32[]{:S(2)}) collective-permute-start(f32[384,256]{1,0:T(8,128)S(1)} %projected.1), channel_id=1, source_target_pairs={{0,1},{1,0},{2,3},{3,2},{4,5},{5,4},{6,7},{7,6},{8,9},{9,8},{10,11... | collective-permute-start | bytes 1179656 | tf_op jit(solution)/shard_map/ppermute | solution.py:274
  48.7 9.0 %collective-permute-start.6 = (bf16[384,256]{1,0:T(8,128)(2,1)S(1)}, bf16[384,256]{1,0:T(8,128)(2,1)S(1)}, u32[]{:S(2)}, u32[]{:S(2)}) collective-permute-start(bf16[384,256]{1,0:T(8,128)(2,1)S(1)} %add_convert_fusion.refs_0_), channel_id=1, source_target_pairs={{0,4},{1,5},{2,6},{3,7},{4,8},{5,9},{6,10},{7,11},{8,12},{9,13},{1... | collective-permute-start | bytes 589832 | tf_op jit(solution)/shard_map/ppermute | solution.py:280
  52.5 8.7 %collective-permute-start.5 = (bf16[384,256]{1,0:T(8,128)(2,1)S(1)}, bf16[384,256]{1,0:T(8,128)(2,1)S(1)}, u32[]{:S(2)}, u32[]{:S(2)}) collective-permute-start(bf16[384,256]{1,0:T(8,128)(2,1)S(1)} %add_convert_fusion.refs_0_), channel_id=1, source_target_pairs={{0,2},{1,3},{2,4},{3,5},{4,6},{5,7},{6,8},{7,9},{8,10},{9,11},{10,... | collective-permute-start | bytes 589832 | tf_op jit(solution)/shard_map/ppermute | solution.py:280
  54.3 6.8 %collective-permute-start.7 = (bf16[384,256]{1,0:T(8,128)(2,1)S(1)}, bf16[384,256]{1,0:T(8,128)(2,1)S(1)}, u32[]{:S(2)}, u32[]{:S(2)}) collective-permute-start(bf16[384,256]{1,0:T(8,128)(2,1)S(1)} %add_convert_fusion.refs_0_), channel_id=1, source_target_pairs={{0,1},{1,0},{2,3},{3,2},{4,5},{5,4},{6,7},{7,6},{8,9},{9,8},{10,11... | collective-permute-start | bytes 589832 | tf_op jit(solution)/shard_map/ppermute | solution.py:274
  57.7 3.4 %collective-permute-start.9 = (bf16[384,256]{1,0:T(8,128)(2,1)S(1)}, bf16[384,256]{1,0:T(8,128)(2,1)S(1)}, u32[]{:S(2)}, u32[]{:S(2)}) collective-permute-start(bf16[384,256]{1,0:T(8,128)(2,1)S(1)} %collective-permute-done.6.refs_2_), channel_id=1, source_target_pairs={{0,1},{1,0},{2,3},{3,2},{4,5},{5,4},{6,7},{7,6},{8,9},{9,8},{10,11... | collective-permute-start | bytes 589832 | tf_op jit(solution)/shard_map/ppermute | solution.py:274
  61.1 1.4 collective-permute-start.8
  84.7 1.8 %collective-permute-start.10 = (bf16[2,384,256]{2,1,0:T(8,128)(2,1)S(1)}, bf16[2,384,256]{2,1,0:T(8,128)(2,1)S(1)}, u32[]{:S(2)}, u32[]{:S(2)}) collective-permute-start(bf16[2,384,256]{2,1,0:T(8,128)(2,1)S(1)} %get-tuple-element.16), channel_id=1, source_target_pairs={{0,1},{1,0},{2,3},{3,2},{4,5},{5,4},{6,7},{7,6},{8,9},{9,8},{10,11... | collective-permute-start | bytes 1179656 | tf_op jit(solution)/shard_map/ppermute | solution.py:274
  86.6 11.1 %collective-permute-start.12 = (bf16[384,256]{1,0:T(8,128)(2,1)S(1)}, bf16[384,256]{1,0:T(8,128)(2,1)S(1)}, u32[]{:S(2)}, u32[]{:S(2)}) collective-permute-start(bf16[384,256]{1,0:T(8,128)(2,1)S(1)} %get-tuple-element.17), channel_id=1, source_target_pairs={{4,0},{5,1},{6,2},{7,3},{8,4},{9,5},{10,6},{11,7},{12,8},{13,9},{1... | collective-permute-start | bytes 589832 | tf_op jit(solution)/shard_map/ppermute | solution.py:280
  87.9 13.8 %collective-permute-start.11 = (bf16[384,256]{1,0:T(8,128)(2,1)S(1)}, bf16[384,256]{1,0:T(8,128)(2,1)S(1)}, u32[]{:S(2)}, u32[]{:S(2)}) collective-permute-start(bf16[384,256]{1,0:T(8,128)(2,1)S(1)} %get-tuple-element.18), channel_id=1, source_target_pairs={{2,0},{3,1},{4,2},{5,3},{6,4},{7,5},{8,6},{9,7},{10,8},{11,9},{12,... | collective-permute-start | bytes 589832 | tf_op jit(solution)/shard_map/ppermute | solution.py:280
  89.2 13.9 %collective-permute-start.13 = (f32[384,256]{1,0:T(8,128)S(1)}, f32[384,256]{1,0:T(8,128)S(1)}, u32[]{:S(2)}, u32[]{:S(2)}) collective-permute-start(f32[384,256]{1,0:T(8,128)S(1)} %get-tuple-element.19.refs_8_), channel_id=1, source_target_pairs={{0,1},{1,0},{2,3},{3,2},{4,5},{5,4},{6,7},{7,6},{8,9},{9,8},{10,11... | collective-permute-start | bytes 1179656 | tf_op jit(solution)/shard_map/ppermute | solution.py:274
  97.7 4.0 %collective-permute-start.15 = (bf16[384,256]{1,0:T(8,128)(2,1)S(1)}, bf16[384,256]{1,0:T(8,128)(2,1)S(1)}, u32[]{:S(2)}, u32[]{:S(2)}) collective-permute-start(bf16[384,256]{1,0:T(8,128)(2,1)S(1)} %collective-permute-done.12.refs_10_), channel_id=1, source_target_pairs={{0,1},{1,0},{2,3},{3,2},{4,5},{5,4},{6,7},{7,6},{8,9},{9,8},{10,11... | collective-permute-start | bytes 589832 | tf_op jit(solution)/shard_map/ppermute | solution.py:274
  101.7 1.4 collective-permute-start.14
